TPU v7x, 32 devices: a whole 2x2x4 slice. The times are simulated.
32 devices in a mesh: row: 8 (over z, y), col: 4 (over x, core).
Axes of the slice: x: 2, y: 2, z: 4, core: 2. Of those that a mesh axis runs over, the one named last changes fastest.
Arguments:
- probes: bfloat16 [32768, 64], P(('row', 'col')), may hold values from -2 to 2
- points: bfloat16 [3, 32768], P(None, ('row', 'col')), may hold values from 0 to 1
- skeleton: bfloat16 [3, 14336], P(None, ('row', 'col')), may hold values from 0 to 1
- leaf_basis: bfloat16 [32768, 64], P(('row', 'col')), may hold values from -0.375 to 0.375
- transfer: bfloat16 [12288, 64], P(('row', 'col')), may hold values from -0.75 to 0.75
- near_list: int32 [8, 4, 2, 64], P('row', 'col'), may hold values from 0 to 31, as said below
- near_count: int32 [8, 4], P('row', 'col'), may hold values from 8 to 64, as said below
- far_list: int32 [8, 4, 2, 128], P('row', 'col'), may hold values from 0 to 55, as said below
- far_count: int32 [8, 4], P('row', 'col'), may hold values from 16 to 128, as said below
Outputs:
- sample: bfloat16 [32768, 64], P(('row', 'col'))
Inputs may be any that keep to these rules, and one draw needn't show every extreme that they name: `near_list`: row entries index the 16 row leaves of the device's row, column entries the 32 column leaves of its column; only the first near_count slots are used. `near_count`: used slots of one device: 64 on some device in every draw, else 64/2, /4 or /8. `far_list`: row entries index the 28 row clusters, column entries the 56 column clusters; both clusters of a slot lie on the same level; only the first far_count slots are used. `far_count`: used slots of one device: 128 on some device in every draw, else 128/2, /4 or /8.
All inputs are finite; a program needn't handle non-finite values.
Results may differ from a plain program's by a relative error of at most 0.02.
Values may be sent and summed in bfloat16 or wider, within the bound.
No kernel may reach another device: no remote copies, remote signals or barrier semaphores. Data moves between devices by JAX's collectives and lax.ppermute only.
A program may use at most 64 MiB of HBM per device.

v0:
```python
import functools
import math

import jax
import jax.numpy as jnp
from jax import lax
from jax.experimental import pallas as pl
from jax.experimental.pallas import tpu as pltpu
from jax.sharding import PartitionSpec as P

LEAF = 256
RANK = 64
SAMPLES = 64
OWN = 4 * LEAF
CLUSTERS = 7
LANES = 128
F32 = jnp.float32
BF16 = jnp.bfloat16
FAR_ROW = OWN // LANES * SAMPLES
COORD_ROW = FAR_ROW + CLUSTERS * SAMPLES // 2
COORD_ROWS = 96
PACKED_ROWS = COORD_ROW + COORD_ROWS
FEATURES = 16
CLASSES = 2
NEAR_UNROLL = 8
FAR_UNROLL = 16
RATE = math.sqrt(3.0) / 0.15
EARLY_UNITS = 1
HERE_UNITS = 1

ANY = pl.BlockSpec(memory_space=pl.ANY)
VMEM = pl.BlockSpec(memory_space=pltpu.VMEM)
SMEM = pl.BlockSpec(memory_space=pltpu.SMEM)
NN = (((1,), (0,)), ((), ()))
NT = (((1,), (1,)), ((), ()))


def dot(a, b, dims=NN):
    return lax.dot_general(a, b, dims, preferred_element_type=F32)


def dot_wide(a, b):
    high = a.astype(BF16)
    low = (a - high.astype(F32)).astype(BF16)
    return dot(high, b) + dot(low, b)


def lanes(a, b):
    return jnp.concatenate([a, b], axis=1)


def rows(*parts):
    return jnp.concatenate(parts, axis=0)


def features(points):
    norm = points * points
    norm = norm[0:1] + norm[1:2] + norm[2:3]
    high = norm.astype(BF16).astype(F32)
    rest = norm - high
    middle = rest.astype(BF16).astype(F32)
    ones = jnp.ones_like(norm)
    return rows(points, high, middle, rest - middle, ones, ones)


def row_side(made):
    ones = made[6:7]
    return rows(-2.0 * made[0:3], ones, ones, ones, made[3:4], made[4:5])


def matern_of(square):
    square = jnp.maximum(square, 1e-14)
    x = (square * lax.rsqrt(square)) * -RATE
    return ((1.0 - x) * jnp.exp(x)).astype(BF16)


def pack_kernel(probes, basis, moves, points, skeleton, packed, coords):
    near = features(points[...].astype(F32))
    far = features(lanes(skeleton[...].astype(F32), jnp.zeros((3, 64), F32)))
    chunks = [near[:, j * LANES : (j + 1) * LANES] for j in range(8)]
    chunks += [far[:, j * LANES : (j + 1) * LANES] for j in range(4)]
    made = rows(*chunks).astype(BF16)
    packed[COORD_ROW:] = made
    coords[...] = made
    leaves = []
    for l in range(4):
        part = slice(l * LEAF, (l + 1) * LEAF)
        leaves.append(dot(basis[:, part], probes[:, part], NT).astype(BF16))
    middle = [
        dot(moves[:, j * 128 : (j + 1) * 128], rows(*leaves[2 * j : 2 * j + 2])).astype(BF16)
        for j in range(2)
    ]
    top = dot(moves[:, 256:384], rows(*middle)).astype(BF16)
    for j in range(8):
        packed[j * SAMPLES : (j + 1) * SAMPLES] = probes[:, j * LANES : (j + 1) * LANES]
    packed[FAR_ROW : FAR_ROW + 64] = lanes(leaves[0], leaves[1])
    packed[FAR_ROW + 64 : FAR_ROW + 128] = lanes(leaves[2], leaves[3])
    packed[FAR_ROW + 128 : FAR_ROW + 192] = lanes(middle[0], middle[1])
    packed[FAR_ROW + 192 : FAR_ROW + 224] = lanes(top[:32], top[32:])


class Plan:
    def __init__(self, near_most, far_most):
        self.near = near_most + NEAR_UNROLL
        self.far = far_most + FAR_UNROLL
        self.far_first = -(-CLASSES * self.near // LANES) * LANES
        self.size = self.far_first + -(-CLASSES * self.far // LANES) * LANES


def iota(shape, axis):
    return lax.broadcasted_iota(jnp.int32, shape, axis)


def tie_kernel(*refs):
    del refs


def tie(x, *others, cost=None):
    return pl.pallas_call(
        tie_kernel,
        out_shape=jax.ShapeDtypeStruct(x.shape, x.dtype),
        in_specs=[ANY] * (1 + len(others)),
        out_specs=ANY,
        input_output_aliases={0: 0},
        compiler_params=pltpu.CompilerParams(vmem_limit_bytes=1 << 20),
        cost_estimate=cost,
        name="tie",
    )(x, *others)


def join_kernel(count, *refs):
    for mine, other, out in zip(refs[:count], refs[count : 2 * count], refs[2 * count :]):
        out[...] = (mine[...].astype(F32) + other[...].astype(F32)).astype(BF16)


def sort_slots(a_device, a_rest, b_device, b_rest, count, per_device, n_col, n_y, most, width):
    slots = a_device.shape[1]
    target = a_device ^ lax.axis_index("col")
    source = b_device ^ lax.axis_index("row")
    remote = target >= 2
    stage = jnp.where(source > 3 * n_y, 2, jnp.where(source > 2 * n_y, 1, 0))
    group = jnp.where(remote, stage, jnp.where(stage == 0, 3, 4))
    alive = iota((1, slots), 1) < count
    group = jnp.where(alive, group, 7)
    row = (target - jnp.where(remote, 2, 0)) * per_device + a_rest
    column = source * per_device + b_rest
    member = jnp.where(iota((8, slots), 0) == group, 1.0, 0.0)
    before = jnp.where(iota((slots, slots), 0) < iota((slots, slots), 1), 1.0, 0.0)
    ahead = dot(member.astype(BF16), before.astype(BF16))
    ahead = jnp.sum(member * ahead, axis=0, keepdims=True)
    sizes = jnp.sum(member, axis=1, keepdims=True)
    ahead += jnp.where(group == 4, sizes[3:4], 0.0)
    ahead += jnp.where((group == 1) | (group == 2), sizes[0:1], 0.0)
    ahead += jnp.where(group == 2, sizes[1:2], 0.0)
    place = jnp.where(alive, jnp.where(remote, 0, most) + ahead.astype(jnp.int32), -1)
    chosen = jnp.where(iota((width, slots), 0) == place, 1.0, 0.0).astype(BF16)
    ones = jnp.ones((6, slots), F32)
    values = rows(row.astype(F32), column.astype(F32), ones).astype(BF16)
    found = dot(values, chosen, NT)
    here = iota((1, width), 1) >= most
    blank = jnp.where(here, 2.0 * per_device, (n_col - 2.0) * per_device)
    made = rows(found[0:1] + blank * (1.0 - found[2:3]), found[1:2])
    return made.astype(jnp.int32), sizes.astype(jnp.int32)


def plan_kernel(n_col, n_y, plan, slots, coords, mate, out, counts, both):
    both[:COORD_ROWS] = coords[...]
    both[COORD_ROWS:] = mate[...]
    near_most, far_most = plan.near - NEAR_UNROLL, plan.far - FAR_UNROLL
    a, b = slots[0:1, :near_most], slots[1:2, :near_most]
    near, near_counts = sort_slots(
        lax.shift_right_logical(a, 2), a & 3, lax.shift_right_logical(b, 2), b & 3,
        slots[4:5, 0:1], 4, n_col, n_y, plan.near, plan.far_first,
    )
    a, b = slots[2:3, :far_most], slots[3:4, :far_most]
    a_device = lax.shift_right_logical(a * 9363, 16)
    b_device = lax.shift_right_logical(b * 9363, 16)
    far, far_counts = sort_slots(
        a_device, a - a_device * CLUSTERS, b_device, b - b_device * CLUSTERS,
        slots[5:6, 0:1], CLUSTERS, n_col, n_y, plan.far, plan.size - plan.far_first,
    )
    out[:, : plan.far_first] = near
    out[:, plan.far_first :] = far
    counts[...] = jnp.where(iota((8, LANES), 1) == 0, near_counts, far_counts)


def row_kernel(n_col, *refs):
    chips, near_row, far_row = refs[:-3], refs[-2], refs[-1]
    empty = jnp.zeros((8, LANES), F32)
    for i in range(n_col):
        first = i % 2 * COORD_ROWS
        slabs = [chips[i // 2][first + 16 * s : first + 16 * s + 16].astype(F32) for s in range(6)]
        near, far = (4 * i, CLUSTERS * i) if i < 2 else (4 * i + 1, CLUSTERS * i + 1)
        for l in range(4):
            for h in range(2):
                made = row_side(slabs[l][8 * h : 8 * h + 8])
                near_row[near + l, h * LANES : (h + 1) * LANES] = rows(made, empty).T.astype(BF16)
        for c in range(4):
            slab = slabs[4 + c // 2]
            made = row_side(slab[8 * (c % 2) : 8 * (c % 2) + 8])
            tall = rows(made, empty).T.astype(BF16)
            far_row[far + 2 * c] = tall[:64]
            if c < 3:
                far_row[far + 2 * c + 1] = tall[64:]
    for blank in (8, 4 * n_col + 1):
        near_row[blank] = jnp.zeros(near_row.shape[1:], BF16)
    for blank in (2 * CLUSTERS, CLUSTERS * n_col + 1):
        far_row[blank] = jnp.zeros(far_row.shape[1:], BF16)


def prepare(i, block, probes, near_col, coeff_low, coeff_high, far_low, far_high):
    for l in range(4):
        for h in range(2):
            j = 2 * l + h
            half = slice(h * LANES, (h + 1) * LANES)
            probes[4 * i + l, :, half] = block[j * SAMPLES : (j + 1) * SAMPLES]
        slab = block[COORD_ROW + 16 * l : COORD_ROW + 16 * (l + 1)]
        near_col[4 * i + l, :, :LANES] = slab
        near_col[4 * i + l, :, LANES:] = rows(slab[8:], slab[:8])
    slabs = [block[COORD_ROW + 64 + 16 * p : COORD_ROW + 80 + 16 * p] for p in range(2)]
    for k in range(CLUSTERS):
        c, half = k // 2, slice(k % 2 * 64, k % 2 * 64 + 64)
        if k < 6:
            own = block[FAR_ROW + 64 * c : FAR_ROW + 64 * (c + 1)][:, half]
        else:
            own = block[FAR_ROW + 192 : FAR_ROW + 224]
            own = rows(own[:, :64], own[:, 64:])
        empty = jnp.zeros_like(own)
        coeff_low[CLUSTERS * i + k] = lanes(own, empty)
        coeff_high[CLUSTERS * i + k] = lanes(empty, own)
        made = slabs[c // 2].astype(F32)[8 * (c % 2) : 8 * (c % 2) + 8, half]
        empty = jnp.zeros_like(made)
        blank = jnp.zeros((8, LANES), F32)
        far_low[CLUSTERS * i + k] = rows(lanes(made, empty), blank).astype(BF16)
        far_high[CLUSTERS * i + k] = rows(lanes(empty, made), blank).astype(BF16)


def work(plan, here, stage, lists, counts, near_row, far_row, prepared, totals):
    probes, near_col, coeff_low, coeff_high, far_low, far_high = prepared
    near_total, far_even, far_odd = totals
    near_first, far_first = (0, 0) if here else (9, 2 * CLUSTERS + 1)

    def near_terms(place, slots):
        terms = []
        for u in range(slots):
            a, b = lists[0, place + u], lists[1, place + u]
            values = matern_of(dot(near_row[near_first + a], near_col[b]))
            terms.append((a, dot(probes[b], values, NT)))
        return terms

    def near_add(terms):
        for a, term in terms:
            near_total[a] += term

    def far_terms(place):
        terms = []
        for u in range(0, FAR_UNROLL, 2):
            a0, a1 = lists[0, place + u], lists[0, place + u + 1]
            b0, b1 = lists[1, place + u], lists[1, place + u + 1]
            square = dot(far_row[far_first + a0], far_low[b0])
            square += dot(far_row[far_first + a1], far_high[b1])
            both = rows(coeff_low[b0], coeff_high[b1])
            terms.append((a0, a1, dot(matern_of(square), both)))
        return terms

    def far_add(terms):
        for a0, a1, term in terms:
            far_even[a0] += term
            far_odd[a1] += term

    half = NEAR_UNROLL // 2

    def bounds(kind, unroll):
        sizes = [counts[k, kind] for k in ((3, 4) if here else (0, 1, 2))]
        ends = [jnp.minimum(sizes[0] // unroll, HERE_UNITS if here else EARLY_UNITS)]
        if not here:
            ends += [sizes[0] // unroll, (sizes[0] + sizes[1]) // unroll]
        first = ends[stage - 1] if stage else 0
        if stage < len(ends):
            return first, (ends[stage] - first) * unroll
        return first, sum(sizes) - first * unroll

    near_from, near_count = bounds(0, NEAR_UNROLL)
    far_from, far_count = bounds(1, FAR_UNROLL)
    halves = (near_count + half - 1) // half
    near_groups = halves // 2
    far_groups = (far_count + FAR_UNROLL - 1) // FAR_UNROLL
    together = jnp.minimum(near_groups, far_groups)
    near_place = here * plan.near + near_from * NEAR_UNROLL
    far_place = plan.far_first + here * plan.far + far_from * FAR_UNROLL

    def joint_step(g, _):
        near = near_terms(near_place + g * NEAR_UNROLL, NEAR_UNROLL)
        far = far_terms(far_place + g * FAR_UNROLL)
        near_add(near)
        far_add(far)
        return 0

    def near_step(g, _):
        near_add(near_terms(near_place + g * NEAR_UNROLL, NEAR_UNROLL))
        return 0

    def far_step(g, _):
        far_add(far_terms(far_place + g * FAR_UNROLL))
        return 0

    lax.fori_loop(0, together, joint_step, 0)
    lax.fori_loop(together, near_groups, near_step, 0)
    lax.fori_loop(together, far_groups, far_step, 0)

    if stage < (1 if here else 3):
        return

    @pl.when(halves % 2 == 1)
    def _():
        near_add(near_terms(near_place + near_groups * NEAR_UNROLL, half))


def write_parts(outs, near_total, far_even, far_odd):
    for i, out in enumerate(outs):
        for j in range(8):
            half = slice(j % 2 * LANES, (j % 2 + 1) * LANES)
            part = near_total[4 * i + j // 2, :, half]
            out[j * SAMPLES : (j + 1) * SAMPLES] = part.astype(BF16)
        parts = []
        for l in range(CLUSTERS):
            even, odd = far_even[CLUSTERS * i + l], far_odd[CLUSTERS * i + l]
            parts.append(even[:, :64] + odd[:, 64:])
        for j in range(3):
            pair = lanes(*parts[2 * j : 2 * j + 2])
            out[FAR_ROW + 64 * j : FAR_ROW + 64 * (j + 1)] = pair.astype(BF16)
        pair = lanes(parts[6][:32], parts[6][32:])
        out[FAR_ROW + 192 : FAR_ROW + 224] = pair.astype(BF16)


def clear(totals):
    for total in totals:
        total[...] = jnp.zeros_like(total)


def early_kernel(plan, copied, members, lists, counts, near_row, far_row, *refs):
    blocks, refs = refs[: len(members)], refs[len(members) :]
    prepared, totals = refs[:6], refs[6:]
    clear(totals)
    for i, block in zip(members, blocks):
        prepare(i, block, *prepared)
    work(plan, 0, 0, lists, counts, near_row, far_row, prepared, totals)


def carry(before, after, copied):
    if copied:
        for old, new in zip(before, after):
            new[...] = old[...]


def second_kernel(plan, copied, members, lists, counts, near_row, far_row, *refs):
    before, refs = refs[:9], refs[9:]
    prepared, totals, here = refs[:6], refs[6:9], refs[9:]
    carry(before, refs, copied)
    clear(here)
    work(plan, 0, 1, lists, counts, near_row, far_row, prepared, totals)
    work(plan, 1, 0, lists, counts, near_row, far_row, prepared, here)


def mid_kernel(plan, copied, members, lists, counts, near_row, far_row, *refs):
    blocks, before, refs = refs[: len(members)], refs[len(members) :][:9], refs[len(members) + 9 :]
    prepared, totals = refs[:6], refs[6:9]
    carry(before, refs, copied)
    for i, block in zip(members, blocks):
        prepare(i, block, *prepared)
    work(plan, 0, 2, lists, counts, near_row, far_row, prepared, totals)


def late_kernel(plan, copied, members, lists, counts, near_row, far_row, *refs):
    blocks, before, refs = refs[: len(members)], refs[len(members) :][:9], refs[len(members) + 9 :]
    prepared, totals, outs = refs[:6], refs[6:9], refs[9:]
    carry(before, refs, copied)
    for i, block in zip(members, blocks):
        prepare(i, block, *prepared)
    work(plan, 0, 3, lists, counts, near_row, far_row, prepared, totals)
    write_parts(outs, *totals)


def here_kernel(plan, copied, lists, counts, near_row, far_row, *refs):
    prepared, before, refs = refs[:6], refs[7:10], refs[10:]
    totals, outs = refs[:3], refs[3:]
    carry(before, refs, copied)
    work(plan, 1, 1, lists, counts, near_row, far_row, prepared, totals)
    write_parts(outs, *totals)


def final_kernel(count, basis, moves, *refs):
    parts, out = refs[:count], refs[count]

    def total(first, count):
        return sum(part[first : first + count].astype(F32) for part in parts)

    def turned(first):
        tall = total(first, 64).T
        return lanes(tall[:64], tall[64:])

    top = total(FAR_ROW + 192, 32)
    top = rows(top[:, :64], top[:, 64:]).T
    middle = turned(FAR_ROW + 128) + dot_wide(top, moves[:, 256:384])
    for j in range(2):
        pair = turned(FAR_ROW + 64 * j) + dot_wide(
            middle[:, j * RANK : (j + 1) * RANK], moves[:, j * 128 : (j + 1) * 128]
        )
        for k in range(2):
            l = 2 * j + k
            expanded = dot_wide(
                pair[:, k * RANK : (k + 1) * RANK], basis[:, l * LEAF : (l + 1) * LEAF]
            )
            for h in range(2):
                place = (2 * l + h) * LANES
                near = total((2 * l + h) * SAMPLES, SAMPLES)
                made = near + expanded[:, h * LANES : (h + 1) * LANES]
                out[:, place : place + LANES] = made.astype(BF16)


def exchange(x, axis, offset):
    size = lax.axis_size(axis)
    return lax.ppermute(x, axis, [(i, i ^ offset) for i in range(size)])


def local(
    probes, points, skeleton, leaf_basis, transfer, near_list, near_count, far_list, far_count
):
    n_row = lax.axis_size("row")
    n_col = lax.axis_size("col")
    n_y = n_row // 4
    probes, basis, moves = probes.T, leaf_basis.T, transfer.T
    inputs = (probes, basis, moves, points, skeleton)
    small = pltpu.CompilerParams(vmem_limit_bytes=8 << 20)
    packed, coords = pl.pallas_call(
        pack_kernel,
        out_shape=[
            jax.ShapeDtypeStruct((PACKED_ROWS, LANES), BF16),
            jax.ShapeDtypeStruct((COORD_ROWS, LANES), BF16),
        ],
        in_specs=[VMEM] * 5,
        out_specs=[VMEM] * 2,
        name="pack",
    )(*inputs)

    plan = Plan(near_list.shape[-1], far_list.shape[-1])
    width = max(LANES, near_list.shape[-1], far_list.shape[-1])

    def placed(x, row):
        return jnp.pad(x, ((row, 8 - row - x.shape[0]), (0, width - x.shape[1])))

    slots = placed(near_list[0, 0], 0) + placed(far_list[0, 0], 2)
    slots = slots + placed(near_count, 4) + placed(far_count, 5)

    def along_z(x, planes, flip):
        pairs = [(z * n_y + y, (z ^ flip) * n_y + y) for z in planes for y in range(n_y)]
        return lax.ppermute(x, "row", pairs)

    own_y = exchange(packed, "row", 1)
    second = along_z(packed, (0, 1, 2, 3), 2)
    neighbour = along_z(packed, (0, 1, 2, 3), 1)
    lists, counts, both = pl.pallas_call(
        functools.partial(plan_kernel, n_col, n_y, plan),
        out_shape=[
            jax.ShapeDtypeStruct((2, plan.size), jnp.int32),
            jax.ShapeDtypeStruct((8, LANES), jnp.int32),
            jax.ShapeDtypeStruct((2 * COORD_ROWS, LANES), BF16),
        ],
        in_specs=[VMEM] * 3,
        out_specs=[VMEM] * 3,
        compiler_params=small,
        cost_estimate=pl.CostEstimate(flops=1 << 30, bytes_accessed=1 << 12, transcendentals=0),
        name="plan",
    )(slots, coords, exchange(coords, "col", 1))

    row_coords = [both] + [exchange(both, "col", k) for k in range(2, n_col, 2)]
    neighbour = tie(neighbour, lists)
    neighbour_y = exchange(neighbour, "row", 1)
    second = tie(second, own_y, neighbour, lists)
    def with_y(block, first=None):
        blocks = [block, exchange(block, "row", 1) if first is None else first]
        return blocks + [exchange(block, "row", y) for y in range(2, n_y)]

    blocks = with_y(packed, own_y) + with_y(neighbour, neighbour_y) + with_y(second)

    row_features = pl.pallas_call(
        functools.partial(row_kernel, n_col),
        out_shape=[
            jax.ShapeDtypeStruct((4 * n_col + 2, LEAF, FEATURES), BF16),
            jax.ShapeDtypeStruct((CLUSTERS * n_col + 2, RANK, FEATURES), BF16),
        ],
        in_specs=[VMEM] * (n_col // 2) + [ANY],
        out_specs=[VMEM] * 2,
        compiler_params=small,
        name="row_side",
    )(*row_coords, second)

    def sums(targets):
        near = (4 * targets + 1, SAMPLES, LEAF)
        far = (CLUSTERS * targets + 1, RANK, LANES)
        return [near, far, far]

    part = jax.ShapeDtypeStruct((COORD_ROW, LANES), BF16)
    held = [
        jax.ShapeDtypeStruct(shape, BF16)
        for shape in [
            (4 * n_row, SAMPLES, LEAF),
            (4 * n_row, FEATURES, LEAF),
            (CLUSTERS * n_row, RANK, LANES),
            (CLUSTERS * n_row, RANK, LANES),
            (CLUSTERS * n_row, FEATURES, LANES),
            (CLUSTERS * n_row, FEATURES, LANES),
        ]
    ]
    held += [jax.ShapeDtypeStruct(shape, F32) for shape in sums(n_col - 2)]
    params = pltpu.CompilerParams(vmem_limit_bytes=32 << 20)
    cost = pl.CostEstimate(flops=1 << 33, bytes_accessed=1 << 20, transcendentals=0)
    local_sums = [jax.ShapeDtypeStruct(shape, F32) for shape in sums(2)]
    copied = sum(math.prod(x.shape) * x.dtype.itemsize for x in held) > 8 << 20

    def stage(kernel, members, out_shape, name):
        first = 4 + len(members)
        return pl.pallas_call(
            functools.partial(kernel, plan, copied, members),
            out_shape=out_shape,
            in_specs=[SMEM] * 2 + [VMEM] * (2 + len(members) + len(handed)),
            out_specs=[VMEM] * len(out_shape),
            input_output_aliases={first + k: k for k in range(len(handed))},
            compiler_params=params,
            cost_estimate=cost,
            name=name,
        )(lists, counts, *row_features, *[blocks[j] for j in members], *handed)

    handed = []
    handed = stage(early_kernel, list(range(2 * n_y + 1)), held, "early")
    third = tie(along_z(second, (0, 1, 2, 3), 1), handed[6])
    blocks += with_y(third)
    both_sums = stage(second_kernel, [], held + local_sums, "second")
    handed, here_totals = both_sums[: len(held)], both_sums[len(held) :]
    handed = stage(mid_kernel, list(range(2 * n_y + 1, 3 * n_y + 1)), held, "mid")
    handed = stage(late_kernel, list(range(3 * n_y + 1, n_row)), held + [part] * (n_col - 2), "late")
    prepared, parts = handed[:6], handed[len(held) :]
    mine, other = parts[0::2], [exchange(part, "col", 1) for part in parts[1::2]]
    joined = pl.pallas_call(
        functools.partial(join_kernel, len(mine)),
        out_shape=[part] * len(mine),
        in_specs=[VMEM] * (2 * len(mine)),
        out_specs=[VMEM] * len(mine),
        compiler_params=params,
        name="join",
    )(*mine, *other)
    arrived = [exchange(joined[k], "col", 2 * k + 2) for k in range(len(mine))]
    here = pl.pallas_call(
        functools.partial(here_kernel, plan, copied),
        out_shape=local_sums + [part] * 2,
        in_specs=[SMEM] * 2 + [VMEM] * 8 + [ANY] + [VMEM] * 3,
        out_specs=[VMEM] * 5,
        input_output_aliases={11 + k: k for k in range(3)},
        compiler_params=params,
        cost_estimate=cost,
        name="here",
    )(lists, counts, *row_features, *prepared, joined[0], *here_totals)[3:]
    arrived = [tie(x, cost=cost) for x in arrived]
    arrived += [here[0], exchange(here[1], "col", 1)]
    sample = pl.pallas_call(
        functools.partial(final_kernel, len(arrived)),
        out_shape=jax.ShapeDtypeStruct((SAMPLES, OWN), BF16),
        in_specs=[VMEM] * (2 + len(arrived)),
        out_specs=VMEM,
        compiler_params=pltpu.CompilerParams(vmem_limit_bytes=16 << 20),
        name="final",
    )(basis, moves, *arrived)
    return sample.T


def solution(mesh):
    placed = (
        P(("row", "col"), None),
        P(None, ("row", "col")),
        P(None, ("row", "col")),
        P(("row", "col"), None),
        P(("row", "col"), None),
        P("row", "col", None, None),
        P("row", "col"),
        P("row", "col", None, None),
        P("row", "col"),
    )
    return jax.shard_map(
        local, mesh=mesh, in_specs=placed, out_specs=P(("row", "col"), None), check_vma=False
    )
```

profile of v0, /device:TPU:0, one launch (start us, length us, event | category | flops | bytes accessed | tf_op | source)
XLA Modules:
  0.0 44.0 jit_solution(13001783433324201319)
XLA Ops:
  0.0 2.2 %pack.1 = (bf16[832,128]{1,0:T(8,128)(2,1)}, bf16[96,128]{1,0:T(8,128)(2,1)}) custom-call(bf16[64,1024]{1,0:T(8,128)(2,1)} %bitcast.10, bf16[64,1024]{1,0:T(8,128)(2,1)} %bitcast.6, bf16[64,384]{1,0:T(8,128)(2,1)} %bitcast.8, bf16[3,1024]{1,0:T(4,128)(2,1)} %points.1, bf16[3,448]{1,0:T(4,128)(2,1)} %skeleton.1), custom_call_target="tpu_custom_call" | custom-call | tf_op jit(solution)/shard_map/pack/pallas_call | solution.py:435
  2.2 3.0 %collective-permute-start.4 = (bf16[832,128]{1,0:T(8,128)(2,1)}, bf16[832,128]{1,0:T(8,128)(2,1)S(1)}, u32[]{:S(2)}, u32[]{:S(2)}) collective-permute-start(bf16[832,128]{1,0:T(8,128)(2,1)} %get-tuple-element.56.refs_0_), channel_id=1, source_target_pairs={{0,8},{4,12},{8,0},{12,4},{16,24},{20,28},{24,16},{28,20},{1,9},{5... | collective-permute-start | bytes 638984 | tf_op jit(solution)/shard_map/ppermute | solution.py:457
  5.2 1.5 %collective-permute-start.3 = (bf16[832,128]{1,0:T(8,128)(2,1)}, bf16[832,128]{1,0:T(8,128)(2,1)S(1)}, u32[]{:S(2)}, u32[]{:S(2)}) collective-permute-start(bf16[832,128]{1,0:T(8,128)(2,1)} %get-tuple-element.56.refs_0_), channel_id=1, source_target_pairs={{0,4},{4,0},{8,12},{12,8},{16,20},{20,16},{24,28},{28,24},{1,5},{5... | collective-permute-start | bytes 638984 | tf_op jit(solution)/shard_map/ppermute | solution.py:423
  6.7 2.6 %collective-permute-start.2 = (bf16[832,128]{1,0:T(8,128)(2,1)}, bf16[832,128]{1,0:T(8,128)(2,1)S(1)}, u32[]{:S(2)}, u32[]{:S(2)}) collective-permute-start(bf16[832,128]{1,0:T(8,128)(2,1)} %get-tuple-element.56.refs_0_), channel_id=1, source_target_pairs={{0,16},{4,20},{8,24},{12,28},{16,0},{20,4},{24,8},{28,12},{1,17},{... | collective-permute-start | bytes 638984 | tf_op jit(solution)/shard_map/ppermute | solution.py:457
  10.6 0.7 %pad_add_fusion.slots = s32[8,128]{1,0:T(8,128)S(1)} fusion(s32[1,1]{1,0:T(1,128)S(6)} %copy.79, s32[1,1]{1,0:T(1,128)S(6)} %copy.78, s32[2,128]{1,0:T(2,128)} %bitcast.11, s32[2,64]{1,0:T(2,128)} %bitcast.12), kind=kLoop, calls=%fused_computation | loop fusion | flops 3072 | bytes 5640 | tf_op jit(solution)/shard_map/add | solution.py:453
  11.3 0.7 %copy-done.3 = bf16[96,128]{1,0:T(8,128)(2,1)S(1)} copy-done((bf16[96,128]{1,0:T(8,128)(2,1)S(1)}, bf16[96,128]{1,0:T(8,128)(2,1)}, u32[]{:S(2)}) %copy-start.3) | copy-done | bytes 24600
  12.1 0.4 plan.1
  12.5 1.0 %collective-permute-done.4.refs_0_ = bf16[832,128]{1,0:T(8,128)(2,1)S(1)} collective-permute-done((bf16[832,128]{1,0:T(8,128)(2,1)}, bf16[832,128]{1,0:T(8,128)(2,1)S(1)}, u32[]{:S(2)}, u32[]{:S(2)}) %collective-permute-start.4) | collective-permute-done | bytes 213024 | tf_op jit(solution)/shard_map/ppermute | solution.py:457
  13.5 3.1 %collective-permute-start.6 = (bf16[832,128]{1,0:T(8,128)(2,1)S(1)}, bf16[832,128]{1,0:T(8,128)(2,1)S(1)}, u32[]{:S(2)}, u32[]{:S(2)}) collective-permute-start(bf16[832,128]{1,0:T(8,128)(2,1)S(1)} %tie.4.refs_2_), channel_id=1, source_target_pairs={{0,4},{4,0},{8,12},{12,8},{16,20},{20,16},{24,28},{28,24},{1,5},{5... | collective-permute-start | bytes 638984 | tf_op jit(solution)/shard_map/ppermute | solution.py:423
  16.6 1.5 %collective-permute-start.1 = (bf16[192,128]{1,0:T(8,128)(2,1)S(1)}, bf16[192,128]{1,0:T(8,128)(2,1)S(1)}, u32[]{:S(2)}, u32[]{:S(2)}) collective-permute-start(bf16[192,128]{1,0:T(8,128)(2,1)S(1)} %get-tuple-element.55.refs_0_), channel_id=1, source_target_pairs={{0,2},{1,3},{2,0},{3,1},{4,6},{5,7},{6,4},{7,5},{8,10},{9,11},{10,... | collective-permute-start | bytes 147464 | tf_op jit(solution)/shard_map/ppermute | solution.py:423
  18.0 0.9 %collective-permute-done.2.refs_0_ = bf16[832,128]{1,0:T(8,128)(2,1)S(1)} collective-permute-done((bf16[832,128]{1,0:T(8,128)(2,1)}, bf16[832,128]{1,0:T(8,128)(2,1)S(1)}, u32[]{:S(2)}, u32[]{:S(2)}) %collective-permute-start.2) | collective-permute-done | bytes 213024 | tf_op jit(solution)/shard_map/ppermute | solution.py:457
  18.9 0.7 %collective-permute-start.8 = (bf16[832,128]{1,0:T(8,128)(2,1)S(1)}, bf16[832,128]{1,0:T(8,128)(2,1)S(1)}, u32[]{:S(2)}, u32[]{:S(2)}) collective-permute-start(bf16[832,128]{1,0:T(8,128)(2,1)S(1)} %tie.5.refs_2_.refs_4_), channel_id=1, source_target_pairs={{0,4},{4,0},{8,12},{12,8},{16,20},{20,16},{24,28},{28,24},{1,5},{5... | collective-permute-start | bytes 638984 | tf_op jit(solution)/shard_map/ppermute | solution.py:423
  19.6 1.0 %collective-permute-done.1.refs_1_ = bf16[192,128]{1,0:T(8,128)(2,1)S(1)} collective-permute-done((bf16[192,128]{1,0:T(8,128)(2,1)S(1)}, bf16[192,128]{1,0:T(8,128)(2,1)S(1)}, u32[]{:S(2)}, u32[]{:S(2)}) %collective-permute-start.1) | collective-permute-done | bytes 49184 | tf_op jit(solution)/shard_map/ppermute | solution.py:423
  20.6 0.5 %row_side.1 = (bf16[18,256,16]{2,1,0:T(8,128)(2,1)S(1)}, bf16[30,64,16]{2,1,0:T(8,128)(2,1)S(1)}) custom-call(bf16[192,128]{1,0:T(8,128)(2,1)S(1)} %get-tuple-element.55.refs_0_, bf16[192,128]{1,0:T(8,128)(2,1)S(1)} %collective-permute-done.1.refs_1_, bf16[832,128]{1,0:T(8,128)(2,1)S(1)} %tie.5.refs_2_.refs_4_), custom_call_target="tpu_custom_call" | custom-call | tf_op jit(solution)/shard_map/row_side/pallas_call | solution.py:486
  21.1 0.4 collective-permute-done.6.refs_3_
  21.5 2.2 %early.1 = (bf16[32,64,256]{2,1,0:T(8,128)(2,1)S(1)}, bf16[32,16,256]{2,1,0:T(8,128)(2,1)S(1)}, bf16[56,64,128]{2,1,0:T(8,128)(2,1)S(1)}, bf16[56,64,128]{2,1,0:...) custom-call(s32[2,640]{1,0:T(2,128)S(1)} %get-tuple-element.53.refs_, ...), custom_call_target="tpu_custom_call" | custom-call | flops 8589934592 | bytes 1048576 | tf_op jit(solution)/shard_map/early/pallas_call | solution.py:523
  23.7 1.0 %collective-permute-done.5.refs_0_ = bf16[832,128]{1,0:T(8,128)(2,1)S(1)} collective-permute-done((bf16[832,128]{1,0:T(8,128)(2,1)S(1)}, bf16[832,128]{1,0:T(8,128)(2,1)S(1)}, u32[]{:S(2)}, u32[]{:S(2)}) %collective-permute-start.5) | collective-permute-done | bytes 213024 | tf_op jit(solution)/shard_map/ppermute | solution.py:457
  24.8 0.6 %collective-permute-start.7 = (bf16[832,128]{1,0:T(8,128)(2,1)S(1)}, bf16[832,128]{1,0:T(8,128)(2,1)S(1)}, u32[]{:S(2)}, u32[]{:S(2)}) collective-permute-start(bf16[832,128]{1,0:T(8,128)(2,1)S(1)} %tie.6.refs_1_), channel_id=1, source_target_pairs={{0,4},{4,0},{8,12},{12,8},{16,20},{20,16},{24,28},{28,24},{1,5},{5... | collective-permute-start | bytes 638984 | tf_op jit(solution)/shard_map/ppermute | solution.py:423
  25.4 1.8 %second.1 = (bf16[32,64,256]{2,1,0:T(8,128)(2,1)S(1)}, bf16[32,16,256]{2,1,0:T(8,128)(2,1)S(1)}, bf16[56,64,128]{2,1,0:T(8,128)(2,1)S(1)}, bf16[56,64,128]{2,1,0...) custom-call(s32[2,640]{1,0:T(2,128)S(1)} %get-tuple-element.53.refs_, ...), custom_call_target="tpu_custom_call", output_to_operand_aliasing={{0}: (4, {}), {1}: (5, {}), {2}: (6, {}), {3}: (7, {}), {4}... | custom-call | flops 8589934592 | bytes 1048576 | tf_op jit(solution)/shard_map/second/pallas_call | solution.py:523
  27.2 1.3 %mid.1 = (bf16[32,64,256]{2,1,0:T(8,128)(2,1)S(1)}, bf16[32,16,256]{2,1,0:T(8,128)(2,1)S(1)}, bf16[56,64,128]{2,1,0:T(8,128)(2,1)S(1)}, bf16[56,64,128]{2,1,0:T(...) custom-call(s32[2,640]{1,0:T(2,128)S(1)} %get-tuple-element.53.refs_, ...), custom_call_target="tpu_custom_call", output_to_operand_aliasing={{0}: (6, {}), {1}: (7, {}), {2}: (8, {}), {3}: (9, {}), {4}... | custom-call | flops 8589934592 | bytes 1048576 | tf_op jit(solution)/shard_map/mid/pallas_call | solution.py:523
  28.4 2.2 %collective-permute-done.7.refs_0_ = bf16[832,128]{1,0:T(8,128)(2,1)S(1)} collective-permute-done((bf16[832,128]{1,0:T(8,128)(2,1)S(1)}, bf16[832,128]{1,0:T(8,128)(2,1)S(1)}, u32[]{:S(2)}, u32[]{:S(2)}) %collective-permute-start.7) | collective-permute-done | bytes 213024 | tf_op jit(solution)/shard_map/ppermute | solution.py:423
  30.6 3.0 %late.1 = (bf16[32,64,256]{2,1,0:T(8,128)(2,1)S(1)}, bf16[32,16,256]{2,1,0:T(8,128)(2,1)S(1)}, bf16[56,64,128]{2,1,0:T(8,128)(2,1)S(1)}, bf16[56,64,128]{2,1,0:T...) custom-call(s32[2,640]{1,0:T(2,128)S(1)} %get-tuple-element.53.refs_, ...), custom_call_target="tpu_custom_call", output_to_operand_aliasing={{0}: (5, {}), {1}: (6, {}), {2}: (7, {}), {3}: (8, {}), {4}... | custom-call | flops 8589934592 | bytes 1048576 | tf_op jit(solution)/shard_map/late/pallas_call | solution.py:523
  33.6 0.1 collective-permute-start.9
  33.7 1.4 %collective-permute-done.9.refs_1_ = bf16[736,128]{1,0:T(8,128)(2,1)S(1)} collective-permute-done((bf16[736,128]{1,0:T(8,128)(2,1)S(1)}, bf16[736,128]{1,0:T(8,128)(2,1)S(1)}, u32[]{:S(2)}, u32[]{:S(2)}) %collective-permute-start.9) | collective-permute-done | bytes 188448 | tf_op jit(solution)/shard_map/ppermute | solution.py:423
  35.1 0.1 join.1.refs_6_
  35.2 2.2 %collective-permute-start.10 = (bf16[736,128]{1,0:T(8,128)(2,1)S(1)}, bf16[736,128]{1,0:T(8,128)(2,1)S(1)}, u32[]{:S(2)}, u32[]{:S(2)}) collective-permute-start(bf16[736,128]{1,0:T(8,128)(2,1)S(1)} %join.1.refs_6_), channel_id=1, source_target_pairs={{0,2},{1,3},{2,0},{3,1},{4,6},{5,7},{6,4},{7,5},{8,10},{9,11},{10,... | collective-permute-start | bytes 565256 | tf_op jit(solution)/shard_map/ppermute | solution.py:423
  37.4 2.1 %here.1 = (f32[9,64,256]{2,1,0:T(8,128)S(1)}, f32[15,64,128]{2,1,0:T(8,128)S(1)}, f32[15,64,128]{2,1,0:T(8,128)S(1)}, bf16[736,128]{1,0:T(8,128)(2,1)S(1)}, bf16[736,128]{1,0:T(8,128)(2,1)S(1)}) custom-call(s32[2,640]{1,0:T(2,128)S(1)} %get-tuple-element.53.refs_1_.refs_3_.lists, ...), custom_call_target="tpu_custom_call", output_to_operand_aliasing={{0}: (11, {}), {1}: (12, {}), {2}: (13, {})} | custom-call | flops 8589934592 | bytes 1048576 | tf_op jit(solution)/shard_map/here/pallas_call | solution.py:553
  39.5 0.0 copy-start
  39.5 2.0 %collective-permute-start.11 = (bf16[736,128]{1,0:T(8,128)(2,1)S(1)}, bf16[736,128]{1,0:T(8,128)(2,1)S(1)}, u32[]{:S(2)}, u32[]{:S(2)}) collective-permute-start(bf16[736,128]{1,0:T(8,128)(2,1)S(1)} %get-tuple-element.98), channel_id=1, source_target_pairs={{0,1},{1,0},{2,3},{3,2},{4,5},{5,4},{6,7},{7,6},{8,9},{9,8},{10,11... | collective-permute-start | bytes 565256 | tf_op jit(solution)/shard_map/ppermute | solution.py:423
  41.5 0.9 %collective-permute-done.10.refs_0_ = bf16[736,128]{1,0:T(8,128)(2,1)S(1)} collective-permute-done((bf16[736,128]{1,0:T(8,128)(2,1)S(1)}, bf16[736,128]{1,0:T(8,128)(2,1)S(1)}, u32[]{:S(2)}, u32[]{:S(2)}) %collective-permute-start.10) | collective-permute-done | bytes 188448 | tf_op jit(solution)/shard_map/ppermute | solution.py:423
  42.4 0.1 collective-permute-done.11.refs_2_
  42.6 1.4 %final.1 = bf16[64,1024]{1,0:T(8,128)(2,1)} custom-call(bf16[64,1024]{1,0:T(8,128)(2,1)S(1)} %bitcast.7, bf16[64,384]{1,0:T(8,128)(2,1)S(1)} %bitcast.9, bf16[736,128]{1,0:T(8,128)(2,1)S(1)} %tie.7.refs_0_, bf16[736,128]{1,0:T(8,128)(2,1)S(1)} %get-tuple-element.97.refs_1_, bf16[736,128]{1,0:T(8,128)(2,1)S(1)} %collective-permute-done.11.refs_2_), custom_call_target="tpu_custom_call" | custom-call | tf_op jit(solution)/shard_map/final/pallas_call | solution.py:565
  (15 shorter events, 0.0 us)
Async XLA Ops:
  2.2 11.3 %collective-permute-start.4 = (bf16[832,128]{1,0:T(8,128)(2,1)}, bf16[832,128]{1,0:T(8,128)(2,1)S(1)}, u32[]{:S(2)}, u32[]{:S(2)}) collective-permute-start(bf16[832,128]{1,0:T(8,128)(2,1)} %get-tuple-element.56.refs_0_), channel_id=1, source_target_pairs={{0,8},{4,12},{8,0},{12,4},{16,24},{20,28},{24,16},{28,20},{1,9},{5... | collective-permute-start | bytes 638984 | tf_op jit(solution)/shard_map/ppermute | solution.py:457
  5.2 12.8 %collective-permute-start.3 = (bf16[832,128]{1,0:T(8,128)(2,1)}, bf16[832,128]{1,0:T(8,128)(2,1)S(1)}, u32[]{:S(2)}, u32[]{:S(2)}) collective-permute-start(bf16[832,128]{1,0:T(8,128)(2,1)} %get-tuple-element.56.refs_0_), channel_id=1, source_target_pairs={{0,4},{4,0},{8,12},{12,8},{16,20},{20,16},{24,28},{28,24},{1,5},{5... | collective-permute-start | bytes 638984 | tf_op jit(solution)/shard_map/ppermute | solution.py:423
  6.7 12.2 %collective-permute-start.2 = (bf16[832,128]{1,0:T(8,128)(2,1)}, bf16[832,128]{1,0:T(8,128)(2,1)S(1)}, u32[]{:S(2)}, u32[]{:S(2)}) collective-permute-start(bf16[832,128]{1,0:T(8,128)(2,1)} %get-tuple-element.56.refs_0_), channel_id=1, source_target_pairs={{0,16},{4,20},{8,24},{12,28},{16,0},{20,4},{24,8},{28,12},{1,17},{... | collective-permute-start | bytes 638984 | tf_op jit(solution)/shard_map/ppermute | solution.py:457
  9.3 2.0 %collective-permute-start = (bf16[96,128]{1,0:T(8,128)(2,1)}, bf16[96,128]{1,0:T(8,128)(2,1)S(1)}, u32[]{:S(2)}, u32[]{:S(2)}) collective-permute-start(bf16[96,128]{1,0:T(8,128)(2,1)} %get-tuple-element.52.coords), channel_id=1, source_target_pairs={{0,1},{1,0},{2,3},{3,2},{4,5},{5,4},{6,7},{7,6},{8,9},{9,8},{10,11... | collective-permute-start | bytes 73736 | tf_op jit(solution)/shard_map/ppermute | solution.py:423
  11.3 0.7 %copy-start.3 = (bf16[96,128]{1,0:T(8,128)(2,1)S(1)}, bf16[96,128]{1,0:T(8,128)(2,1)}, u32[]{:S(2)}) copy-start(bf16[96,128]{1,0:T(8,128)(2,1)} %get-tuple-element.52.coords) | copy-start | bytes 73732
  12.4 9.1 %copy-start.2 = (bf16[832,128]{1,0:T(8,128)(2,1)S(1)}, bf16[832,128]{1,0:T(8,128)(2,1)}, u32[]{:S(2)}) copy-start(bf16[832,128]{1,0:T(8,128)(2,1)} %get-tuple-element.56.refs_0_) | copy-start | bytes 638980
  13.5 8.0 %collective-permute-start.6 = (bf16[832,128]{1,0:T(8,128)(2,1)S(1)}, bf16[832,128]{1,0:T(8,128)(2,1)S(1)}, u32[]{:S(2)}, u32[]{:S(2)}) collective-permute-start(bf16[832,128]{1,0:T(8,128)(2,1)S(1)} %tie.4.refs_2_), channel_id=1, source_target_pairs={{0,4},{4,0},{8,12},{12,8},{16,20},{20,16},{24,28},{28,24},{1,5},{5... | collective-permute-start | bytes 638984 | tf_op jit(solution)/shard_map/ppermute | solution.py:423
  16.6 4.1 %collective-permute-start.1 = (bf16[192,128]{1,0:T(8,128)(2,1)S(1)}, bf16[192,128]{1,0:T(8,128)(2,1)S(1)}, u32[]{:S(2)}, u32[]{:S(2)}) collective-permute-start(bf16[192,128]{1,0:T(8,128)(2,1)S(1)} %get-tuple-element.55.refs_0_), channel_id=1, source_target_pairs={{0,2},{1,3},{2,0},{3,1},{4,6},{5,7},{6,4},{7,5},{8,10},{9,11},{10,... | collective-permute-start | bytes 147464 | tf_op jit(solution)/shard_map/ppermute | solution.py:423
  18.9 5.8 %collective-permute-start.5 = (bf16[832,128]{1,0:T(8,128)(2,1)S(1)}, bf16[832,128]{1,0:T(8,128)(2,1)S(1)}, u32[]{:S(2)}, u32[]{:S(2)}) collective-permute-start(bf16[832,128]{1,0:T(8,128)(2,1)S(1)} %tie.5.refs_2_.refs_4_), channel_id=1, source_target_pairs={{0,8},{4,12},{8,0},{12,4},{16,24},{20,28},{24,16},{28,20},{1,9},{5... | collective-permute-start | bytes 638984 | tf_op jit(solution)/shard_map/ppermute | solution.py:457
  18.9 8.3 %collective-permute-start.8 = (bf16[832,128]{1,0:T(8,128)(2,1)S(1)}, bf16[832,128]{1,0:T(8,128)(2,1)S(1)}, u32[]{:S(2)}, u32[]{:S(2)}) collective-permute-start(bf16[832,128]{1,0:T(8,128)(2,1)S(1)} %tie.5.refs_2_.refs_4_), channel_id=1, source_target_pairs={{0,4},{4,0},{8,12},{12,8},{16,20},{20,16},{24,28},{28,24},{1,5},{5... | collective-permute-start | bytes 638984 | tf_op jit(solution)/shard_map/ppermute | solution.py:423
  24.8 5.8 %collective-permute-start.7 = (bf16[832,128]{1,0:T(8,128)(2,1)S(1)}, bf16[832,128]{1,0:T(8,128)(2,1)S(1)}, u32[]{:S(2)}, u32[]{:S(2)}) collective-permute-start(bf16[832,128]{1,0:T(8,128)(2,1)S(1)} %tie.6.refs_1_), channel_id=1, source_target_pairs={{0,4},{4,0},{8,12},{12,8},{16,20},{20,16},{24,28},{28,24},{1,5},{5... | collective-permute-start | bytes 638984 | tf_op jit(solution)/shard_map/ppermute | solution.py:423
  33.6 1.5 %collective-permute-start.9 = (bf16[736,128]{1,0:T(8,128)(2,1)S(1)}, bf16[736,128]{1,0:T(8,128)(2,1)S(1)}, u32[]{:S(2)}, u32[]{:S(2)}) collective-permute-start(bf16[736,128]{1,0:T(8,128)(2,1)S(1)} %get-tuple-element.87), channel_id=1, source_target_pairs={{0,1},{1,0},{2,3},{3,2},{4,5},{5,4},{6,7},{7,6},{8,9},{9,8},{10,11... | collective-permute-start | bytes 565256 | tf_op jit(solution)/shard_map/ppermute | solution.py:423
  35.2 7.3 %collective-permute-start.10 = (bf16[736,128]{1,0:T(8,128)(2,1)S(1)}, bf16[736,128]{1,0:T(8,128)(2,1)S(1)}, u32[]{:S(2)}, u32[]{:S(2)}) collective-permute-start(bf16[736,128]{1,0:T(8,128)(2,1)S(1)} %join.1.refs_6_), channel_id=1, source_target_pairs={{0,2},{1,3},{2,0},{3,1},{4,6},{5,7},{6,4},{7,5},{8,10},{9,11},{10,... | collective-permute-start | bytes 565256 | tf_op jit(solution)/shard_map/ppermute | solution.py:423
  39.5 3.0 %copy-start = (bf16[1024,64]{0,1:T(8,128)(2,1)S(1)}, bf16[1024,64]{0,1:T(8,128)(2,1)}, u32[]{:S(2)}) copy-start(bf16[1024,64]{0,1:T(8,128)(2,1)} %param.12) | copy-start | bytes 393220
  39.5 3.0 %copy-start.1 = (bf16[384,64]{0,1:T(8,128)(2,1)S(1)}, bf16[384,64]{0,1:T(8,128)(2,1)}, u32[]{:S(2)}) copy-start(bf16[384,64]{0,1:T(8,128)(2,1)} %param.13) | copy-start | bytes 147460
  39.5 3.0 %collective-permute-start.11 = (bf16[736,128]{1,0:T(8,128)(2,1)S(1)}, bf16[736,128]{1,0:T(8,128)(2,1)S(1)}, u32[]{:S(2)}, u32[]{:S(2)}) collective-permute-start(bf16[736,128]{1,0:T(8,128)(2,1)S(1)} %get-tuple-element.98), channel_id=1, source_target_pairs={{0,1},{1,0},{2,3},{3,2},{4,5},{5,4},{6,7},{7,6},{8,9},{9,8},{10,11... | collective-permute-start | bytes 565256 | tf_op jit(solution)/shard_map/ppermute | solution.py:423
where the time goes:
time: 43.6 us; the launch traced here: 44 us
  starting transfers between devices  17.2 us (39%)
  Pallas kernels  14.9 us (34%)
  waiting for transfers between devices  9.02 us (21%)
  between operations  1.41 us (3%)
  local copies, waits for them, and re-layouts  0.75 us (2%)
  other arithmetic  0.71 us (2%)
    ppermute x9, starting transfers between devices, exchange(): return lax.ppermute(x, axis, [(i, i ^ offset) for i in range(size)])  11.6 us
    pallas_call x4, Pallas kernels, stage(): pl.pallas_call(functools.partial(kernel, plan, copied, members), out_shap...  8.24 us
    ppermute x9, waiting for transfers between devices, exchange(): return lax.ppermute(x, axis, [(i, i ^ offset) for i in range(size)])  6.1 us
    ppermute x3, starting transfers between devices, along_z(): return lax.ppermute(x, 'row', pairs)  5.62 us
    ppermute x3, waiting for transfers between devices, along_z(): return lax.ppermute(x, 'row', pairs)  2.92 us
    pallas_call x1, Pallas kernels, local(): pl.pallas_call(pack_kernel, out_shape=[jax.ShapeDtypeStruct((PACKED_ROWS,...  2.17 us
    pallas_call x1, Pallas kernels, local(): pl.pallas_call(functools.partial(here_kernel, plan, copied), out_shape=lo...  2.12 us
    pallas_call x1, Pallas kernels, local(): pl.pallas_call(functools.partial(final_kernel, len(arrived)), out_shape=j...  1.44 us
  transfers between devices with their start and end apart: 12, of which 9 were waited for; matrix products, arithmetic and copies ran while one was open for 2% of the time, Pallas kernels for 19%

commit v1 on v0

--- a/solution.py
+++ b/solution.py
@@ -240,33 +240,19 @@
     near_total, far_even, far_odd = totals
     near_first, far_first = (0, 0) if here else (9, 2 * CLUSTERS + 1)
 
-    def near_terms(place, slots):
-        terms = []
-        for u in range(slots):
-            a, b = lists[0, place + u], lists[1, place + u]
-            values = matern_of(dot(near_row[near_first + a], near_col[b]))
-            terms.append((a, dot(probes[b], values, NT)))
-        return terms
-
-    def near_add(terms):
-        for a, term in terms:
-            near_total[a] += term
-
-    def far_terms(place):
-        terms = []
-        for u in range(0, FAR_UNROLL, 2):
-            a0, a1 = lists[0, place + u], lists[0, place + u + 1]
-            b0, b1 = lists[1, place + u], lists[1, place + u + 1]
-            square = dot(far_row[far_first + a0], far_low[b0])
-            square += dot(far_row[far_first + a1], far_high[b1])
-            both = rows(coeff_low[b0], coeff_high[b1])
-            terms.append((a0, a1, dot(matern_of(square), both)))
-        return terms
-
-    def far_add(terms):
-        for a0, a1, term in terms:
-            far_even[a0] += term
-            far_odd[a1] += term
+    def near_slot(place):
+        a, b = lists[0, place], lists[1, place]
+        values = matern_of(dot(near_row[near_first + a], near_col[b]))
+        near_total[a] += dot(probes[b], values, NT)
+
+    def far_pair(place):
+        a0, a1 = lists[0, place], lists[0, place + 1]
+        b0, b1 = lists[1, place], lists[1, place + 1]
+        square = dot(far_row[far_first + a0], far_low[b0])
+        square += dot(far_row[far_first + a1], far_high[b1])
+        term = dot(matern_of(square), rows(coeff_low[b0], coeff_high[b1]))
+        far_even[a0] += term
+        far_odd[a1] += term
 
     half = NEAR_UNROLL // 2
 
@@ -290,18 +276,19 @@
     far_place = plan.far_first + here * plan.far + far_from * FAR_UNROLL
 
     def joint_step(g, _):
-        near = near_terms(near_place + g * NEAR_UNROLL, NEAR_UNROLL)
-        far = far_terms(far_place + g * FAR_UNROLL)
-        near_add(near)
-        far_add(far)
+        for u in range(NEAR_UNROLL):
+            near_slot(near_place + g * NEAR_UNROLL + u)
+            far_pair(far_place + g * FAR_UNROLL + 2 * u)
         return 0
 
     def near_step(g, _):
-        near_add(near_terms(near_place + g * NEAR_UNROLL, NEAR_UNROLL))
+        for u in range(NEAR_UNROLL):
+            near_slot(near_place + g * NEAR_UNROLL + u)
         return 0
 
     def far_step(g, _):
-        far_add(far_terms(far_place + g * FAR_UNROLL))
+        for u in range(0, FAR_UNROLL, 2):
+            far_pair(far_place + g * FAR_UNROLL + u)
         return 0
 
     lax.fori_loop(0, together, joint_step, 0)
@@ -313,7 +300,8 @@
 
     @pl.when(halves % 2 == 1)
     def _():
-        near_add(near_terms(near_place + near_groups * NEAR_UNROLL, half))
+        for u in range(half):
+            near_slot(near_place + near_groups * NEAR_UNROLL + u)
 
 
 def write_parts(outs, near_total, far_even, far_odd):

time: 43.6 us -> 43 us (0.986); the launches traced: 44 us -> 42.7 us
  starting transfers between devices: 17.2 us -> 15.9 us
    pallas_call x4, Pallas kernels: 8.24 us -> 6.82 us  [stage(): pl.pallas_call(functools.partial(kernel, plan, copied, members), out_shap...]
    ppermute x9, starting transfers between devices: 11.6 us -> 10.3 us  [exchange(): return lax.ppermute(x, axis, [(i, i ^ offset) for i in range(size)])]
    pallas_call x1, Pallas kernels: 2.12 us -> 3.28 us  [local(): pl.pallas_call(functools.partial(here_kernel, plan, copied), out_shape=lo...]
    ppermute x3, waiting for transfers between devices: 2.92 us -> 3.47 us  [along_z(): return lax.ppermute(x, 'row', pairs)]
  transfers between devices with their start and end apart: 12 -> 12, of which waited for: 9 -> 8; matrix products, arithmetic and copies ran while one was open for 2% -> 2% of each run, Pallas kernels for 19% -> 20%
where the time goes in v1:
time: 43 us; the launch traced here: 42.7 us
  starting transfers between devices  15.9 us (37%)
  Pallas kernels  14.6 us (34%)
  waiting for transfers between devices  9.37 us (22%)
  between operations  1.41 us (3%)
  local copies, waits for them, and re-layouts  0.75 us (2%)
  other arithmetic  0.71 us (2%)
    ppermute x9, starting transfers between devices, exchange(): return lax.ppermute(x, axis, [(i, i ^ offset) for i in range(size)])  10.3 us
    pallas_call x4, Pallas kernels, stage(): pl.pallas_call(functools.partial(kernel, plan, copied, members), out_shap...  6.82 us
    ppermute x9, waiting for transfers between devices, exchange(): return lax.ppermute(x, axis, [(i, i ^ offset) for i in range(size)])  5.9 us
    ppermute x3, starting transfers between devices, along_z(): return lax.ppermute(x, 'row', pairs)  5.62 us
    ppermute x3, waiting for transfers between devices, along_z(): return lax.ppermute(x, 'row', pairs)  3.47 us
    pallas_call x1, Pallas kernels, local(): pl.pallas_call(functools.partial(here_kernel, plan, copied), out_shape=lo...  3.28 us
    pallas_call x1, Pallas kernels, local(): pl.pallas_call(pack_kernel, out_shape=[jax.ShapeDtypeStruct((PACKED_ROWS,...  2.17 us
    pallas_call x1, Pallas kernels, local(): pl.pallas_call(functools.partial(final_kernel, len(arrived)), out_shape=j...  1.44 us
  transfers between devices with their start and end apart: 12, of which 8 were waited for; matrix products, arithmetic and copies ran while one was open for 2% of the time, Pallas kernels for 20%

profile of v1, /device:TPU:0, one launch (start us, length us, event | category | flops | bytes accessed | tf_op | source)
XLA Modules:
  0.0 42.7 jit_solution(17706322440594406715)
XLA Ops:
  0.0 2.2 %pack.1 = (bf16[832,128]{1,0:T(8,128)(2,1)}, bf16[96,128]{1,0:T(8,128)(2,1)}) custom-call(bf16[64,1024]{1,0:T(8,128)(2,1)} %bitcast.10, bf16[64,1024]{1,0:T(8,128)(2,1)} %bitcast.6, bf16[64,384]{1,0:T(8,128)(2,1)} %bitcast.8, bf16[3,1024]{1,0:T(4,128)(2,1)} %points.1, bf16[3,448]{1,0:T(4,128)(2,1)} %skeleton.1), custom_call_target="tpu_custom_call" | custom-call | tf_op jit(solution)/shard_map/pack/pallas_call | solution.py:423
  2.2 3.0 %collective-permute-start.4 = (bf16[832,128]{1,0:T(8,128)(2,1)}, bf16[832,128]{1,0:T(8,128)(2,1)S(1)}, u32[]{:S(2)}, u32[]{:S(2)}) collective-permute-start(bf16[832,128]{1,0:T(8,128)(2,1)} %get-tuple-element.56.refs_0_), channel_id=1, source_target_pairs={{0,8},{4,12},{8,0},{12,4},{16,24},{20,28},{24,16},{28,20},{1,9},{5... | collective-permute-start | bytes 638984 | tf_op jit(solution)/shard_map/ppermute | solution.py:445
  5.2 1.5 %collective-permute-start.3 = (bf16[832,128]{1,0:T(8,128)(2,1)}, bf16[832,128]{1,0:T(8,128)(2,1)S(1)}, u32[]{:S(2)}, u32[]{:S(2)}) collective-permute-start(bf16[832,128]{1,0:T(8,128)(2,1)} %get-tuple-element.56.refs_0_), channel_id=1, source_target_pairs={{0,4},{4,0},{8,12},{12,8},{16,20},{20,16},{24,28},{28,24},{1,5},{5... | collective-permute-start | bytes 638984 | tf_op jit(solution)/shard_map/ppermute | solution.py:411
  6.7 2.6 %collective-permute-start.2 = (bf16[832,128]{1,0:T(8,128)(2,1)}, bf16[832,128]{1,0:T(8,128)(2,1)S(1)}, u32[]{:S(2)}, u32[]{:S(2)}) collective-permute-start(bf16[832,128]{1,0:T(8,128)(2,1)} %get-tuple-element.56.refs_0_), channel_id=1, source_target_pairs={{0,16},{4,20},{8,24},{12,28},{16,0},{20,4},{24,8},{28,12},{1,17},{... | collective-permute-start | bytes 638984 | tf_op jit(solution)/shard_map/ppermute | solution.py:445
  10.6 0.7 %pad_add_fusion.slots = s32[8,128]{1,0:T(8,128)S(1)} fusion(s32[1,1]{1,0:T(1,128)S(6)} %copy.79, s32[1,1]{1,0:T(1,128)S(6)} %copy.78, s32[2,128]{1,0:T(2,128)} %bitcast.11, s32[2,64]{1,0:T(2,128)} %bitcast.12), kind=kLoop, calls=%fused_computation | loop fusion | flops 3072 | bytes 5640 | tf_op jit(solution)/shard_map/add | solution.py:441
  11.3 0.0 copy-start.3
  11.3 0.7 %copy-done.3 = bf16[96,128]{1,0:T(8,128)(2,1)S(1)} copy-done((bf16[96,128]{1,0:T(8,128)(2,1)S(1)}, bf16[96,128]{1,0:T(8,128)(2,1)}, u32[]{:S(2)}) %copy-start.3) | copy-done | bytes 24600
  12.1 0.4 plan.1
  12.5 1.0 %collective-permute-done.4.refs_0_ = bf16[832,128]{1,0:T(8,128)(2,1)S(1)} collective-permute-done((bf16[832,128]{1,0:T(8,128)(2,1)}, bf16[832,128]{1,0:T(8,128)(2,1)S(1)}, u32[]{:S(2)}, u32[]{:S(2)}) %collective-permute-start.4) | collective-permute-done | bytes 213024 | tf_op jit(solution)/shard_map/ppermute | solution.py:445
  13.5 3.1 %collective-permute-start.6 = (bf16[832,128]{1,0:T(8,128)(2,1)S(1)}, bf16[832,128]{1,0:T(8,128)(2,1)S(1)}, u32[]{:S(2)}, u32[]{:S(2)}) collective-permute-start(bf16[832,128]{1,0:T(8,128)(2,1)S(1)} %tie.4.refs_2_), channel_id=1, source_target_pairs={{0,4},{4,0},{8,12},{12,8},{16,20},{20,16},{24,28},{28,24},{1,5},{5... | collective-permute-start | bytes 638984 | tf_op jit(solution)/shard_map/ppermute | solution.py:411
  16.6 1.5 %collective-permute-start.1 = (bf16[192,128]{1,0:T(8,128)(2,1)S(1)}, bf16[192,128]{1,0:T(8,128)(2,1)S(1)}, u32[]{:S(2)}, u32[]{:S(2)}) collective-permute-start(bf16[192,128]{1,0:T(8,128)(2,1)S(1)} %get-tuple-element.55.refs_0_), channel_id=1, source_target_pairs={{0,2},{1,3},{2,0},{3,1},{4,6},{5,7},{6,4},{7,5},{8,10},{9,11},{10,... | collective-permute-start | bytes 147464 | tf_op jit(solution)/shard_map/ppermute | solution.py:411
  18.0 0.9 %collective-permute-done.2.refs_0_ = bf16[832,128]{1,0:T(8,128)(2,1)S(1)} collective-permute-done((bf16[832,128]{1,0:T(8,128)(2,1)}, bf16[832,128]{1,0:T(8,128)(2,1)S(1)}, u32[]{:S(2)}, u32[]{:S(2)}) %collective-permute-start.2) | collective-permute-done | bytes 213024 | tf_op jit(solution)/shard_map/ppermute | solution.py:445
  18.9 0.7 %collective-permute-start.8 = (bf16[832,128]{1,0:T(8,128)(2,1)S(1)}, bf16[832,128]{1,0:T(8,128)(2,1)S(1)}, u32[]{:S(2)}, u32[]{:S(2)}) collective-permute-start(bf16[832,128]{1,0:T(8,128)(2,1)S(1)} %tie.5.refs_2_.refs_4_), channel_id=1, source_target_pairs={{0,4},{4,0},{8,12},{12,8},{16,20},{20,16},{24,28},{28,24},{1,5},{5... | collective-permute-start | bytes 638984 | tf_op jit(solution)/shard_map/ppermute | solution.py:411
  19.6 1.0 %collective-permute-done.1.refs_1_ = bf16[192,128]{1,0:T(8,128)(2,1)S(1)} collective-permute-done((bf16[192,128]{1,0:T(8,128)(2,1)S(1)}, bf16[192,128]{1,0:T(8,128)(2,1)S(1)}, u32[]{:S(2)}, u32[]{:S(2)}) %collective-permute-start.1) | collective-permute-done | bytes 49184 | tf_op jit(solution)/shard_map/ppermute | solution.py:411
  20.6 0.5 %row_side.1 = (bf16[18,256,16]{2,1,0:T(8,128)(2,1)S(1)}, bf16[30,64,16]{2,1,0:T(8,128)(2,1)S(1)}) custom-call(bf16[192,128]{1,0:T(8,128)(2,1)S(1)} %get-tuple-element.55.refs_0_, bf16[192,128]{1,0:T(8,128)(2,1)S(1)} %collective-permute-done.1.refs_1_, bf16[832,128]{1,0:T(8,128)(2,1)S(1)} %tie.5.refs_2_.refs_4_), custom_call_target="tpu_custom_call" | custom-call | tf_op jit(solution)/shard_map/row_side/pallas_call | solution.py:474
  21.1 0.4 collective-permute-done.6.refs_3_
  21.5 1.6 %early.1 = (bf16[32,64,256]{2,1,0:T(8,128)(2,1)S(1)}, bf16[32,16,256]{2,1,0:T(8,128)(2,1)S(1)}, bf16[56,64,128]{2,1,0:T(8,128)(2,1)S(1)}, bf16[56,64,128]{2,1,0:...) custom-call(s32[2,640]{1,0:T(2,128)S(1)} %get-tuple-element.53.refs_, ...), custom_call_target="tpu_custom_call" | custom-call | flops 8589934592 | bytes 1048576 | tf_op jit(solution)/shard_map/early/pallas_call | solution.py:511
  23.2 1.6 %collective-permute-done.5.refs_0_ = bf16[832,128]{1,0:T(8,128)(2,1)S(1)} collective-permute-done((bf16[832,128]{1,0:T(8,128)(2,1)S(1)}, bf16[832,128]{1,0:T(8,128)(2,1)S(1)}, u32[]{:S(2)}, u32[]{:S(2)}) %collective-permute-start.5) | collective-permute-done | bytes 213024 | tf_op jit(solution)/shard_map/ppermute | solution.py:445
  24.8 1.7 %collective-permute-start.7 = (bf16[832,128]{1,0:T(8,128)(2,1)S(1)}, bf16[832,128]{1,0:T(8,128)(2,1)S(1)}, u32[]{:S(2)}, u32[]{:S(2)}) collective-permute-start(bf16[832,128]{1,0:T(8,128)(2,1)S(1)} %tie.6.refs_1_), channel_id=1, source_target_pairs={{0,4},{4,0},{8,12},{12,8},{16,20},{20,16},{24,28},{28,24},{1,5},{5... | collective-permute-start | bytes 638984 | tf_op jit(solution)/shard_map/ppermute | solution.py:411
  26.4 1.6 %second.1 = (bf16[32,64,256]{2,1,0:T(8,128)(2,1)S(1)}, bf16[32,16,256]{2,1,0:T(8,128)(2,1)S(1)}, bf16[56,64,128]{2,1,0:T(8,128)(2,1)S(1)}, bf16[56,64,128]{2,1,0...) custom-call(s32[2,640]{1,0:T(2,128)S(1)} %get-tuple-element.53.refs_, ...), custom_call_target="tpu_custom_call", output_to_operand_aliasing={{0}: (4, {}), {1}: (5, {}), {2}: (6, {}), {3}: (7, {}), {4}... | custom-call | flops 8589934592 | bytes 1048576 | tf_op jit(solution)/shard_map/second/pallas_call | solution.py:511
  28.1 1.2 %mid.1 = (bf16[32,64,256]{2,1,0:T(8,128)(2,1)S(1)}, bf16[32,16,256]{2,1,0:T(8,128)(2,1)S(1)}, bf16[56,64,128]{2,1,0:T(8,128)(2,1)S(1)}, bf16[56,64,128]{2,1,0:T(...) custom-call(s32[2,640]{1,0:T(2,128)S(1)} %get-tuple-element.53.refs_, ...), custom_call_target="tpu_custom_call", output_to_operand_aliasing={{0}: (6, {}), {1}: (7, {}), {2}: (8, {}), {3}: (9, {}), {4}... | custom-call | flops 8589934592 | bytes 1048576 | tf_op jit(solution)/shard_map/mid/pallas_call | solution.py:511
  29.3 1.3 %collective-permute-done.7.refs_0_ = bf16[832,128]{1,0:T(8,128)(2,1)S(1)} collective-permute-done((bf16[832,128]{1,0:T(8,128)(2,1)S(1)}, bf16[832,128]{1,0:T(8,128)(2,1)S(1)}, u32[]{:S(2)}, u32[]{:S(2)}) %collective-permute-start.7) | collective-permute-done | bytes 213024 | tf_op jit(solution)/shard_map/ppermute | solution.py:411
  30.6 2.3 %late.1 = (bf16[32,64,256]{2,1,0:T(8,128)(2,1)S(1)}, bf16[32,16,256]{2,1,0:T(8,128)(2,1)S(1)}, bf16[56,64,128]{2,1,0:T(8,128)(2,1)S(1)}, bf16[56,64,128]{2,1,0:T...) custom-call(s32[2,640]{1,0:T(2,128)S(1)} %get-tuple-element.53.refs_, ...), custom_call_target="tpu_custom_call", output_to_operand_aliasing={{0}: (5, {}), {1}: (6, {}), {2}: (7, {}), {3}: (8, {}), {4}... | custom-call | flops 8589934592 | bytes 1048576 | tf_op jit(solution)/shard_map/late/pallas_call | solution.py:511
  32.9 0.1 collective-permute-start.9
  33.0 1.4 %collective-permute-done.9.refs_1_ = bf16[736,128]{1,0:T(8,128)(2,1)S(1)} collective-permute-done((bf16[736,128]{1,0:T(8,128)(2,1)S(1)}, bf16[736,128]{1,0:T(8,128)(2,1)S(1)}, u32[]{:S(2)}, u32[]{:S(2)}) %collective-permute-start.9) | collective-permute-done | bytes 188448 | tf_op jit(solution)/shard_map/ppermute | solution.py:411
  34.4 0.1 join.1.refs_6_
  34.4 1.7 %collective-permute-start.10 = (bf16[736,128]{1,0:T(8,128)(2,1)S(1)}, bf16[736,128]{1,0:T(8,128)(2,1)S(1)}, u32[]{:S(2)}, u32[]{:S(2)}) collective-permute-start(bf16[736,128]{1,0:T(8,128)(2,1)S(1)} %join.1.refs_6_), channel_id=1, source_target_pairs={{0,2},{1,3},{2,0},{3,1},{4,6},{5,7},{6,4},{7,5},{8,10},{9,11},{10,... | collective-permute-start | bytes 565256 | tf_op jit(solution)/shard_map/ppermute | solution.py:411
  36.1 3.3 %here.1 = (f32[9,64,256]{2,1,0:T(8,128)S(1)}, f32[15,64,128]{2,1,0:T(8,128)S(1)}, f32[15,64,128]{2,1,0:T(8,128)S(1)}, bf16[736,128]{1,0:T(8,128)(2,1)S(1)}, bf16[736,128]{1,0:T(8,128)(2,1)S(1)}) custom-call(s32[2,640]{1,0:T(2,128)S(1)} %get-tuple-element.53.refs_1_.refs_3_.lists, ...), custom_call_target="tpu_custom_call", output_to_operand_aliasing={{0}: (11, {}), {1}: (12, {}), {2}: (13, {})} | custom-call | flops 8589934592 | bytes 1048576 | tf_op jit(solution)/shard_map/here/pallas_call | solution.py:541
  39.4 0.0 copy-start
  39.5 0.1 collective-permute-start.11
  39.5 1.7 %collective-permute-done.10.refs_0_ = bf16[736,128]{1,0:T(8,128)(2,1)S(1)} collective-permute-done((bf16[736,128]{1,0:T(8,128)(2,1)S(1)}, bf16[736,128]{1,0:T(8,128)(2,1)S(1)}, u32[]{:S(2)}, u32[]{:S(2)}) %collective-permute-start.10) | collective-permute-done | bytes 188448 | tf_op jit(solution)/shard_map/ppermute | solution.py:411
  41.3 1.4 %final.1 = bf16[64,1024]{1,0:T(8,128)(2,1)} custom-call(bf16[64,1024]{1,0:T(8,128)(2,1)S(1)} %bitcast.7, bf16[64,384]{1,0:T(8,128)(2,1)S(1)} %bitcast.9, bf16[736,128]{1,0:T(8,128)(2,1)S(1)} %tie.7.refs_0_, bf16[736,128]{1,0:T(8,128)(2,1)S(1)} %get-tuple-element.97.refs_1_, bf16[736,128]{1,0:T(8,128)(2,1)S(1)} %collective-permute-done.11.refs_2_), custom_call_target="tpu_custom_call" | custom-call | tf_op jit(solution)/shard_map/final/pallas_call | solution.py:553
  (15 shorter events, 0.0 us)
Async XLA Ops:
  2.2 11.3 %collective-permute-start.4 = (bf16[832,128]{1,0:T(8,128)(2,1)}, bf16[832,128]{1,0:T(8,128)(2,1)S(1)}, u32[]{:S(2)}, u32[]{:S(2)}) collective-permute-start(bf16[832,128]{1,0:T(8,128)(2,1)} %get-tuple-element.56.refs_0_), channel_id=1, source_target_pairs={{0,8},{4,12},{8,0},{12,4},{16,24},{20,28},{24,16},{28,20},{1,9},{5... | collective-permute-start | bytes 638984 | tf_op jit(solution)/shard_map/ppermute | solution.py:445
  5.2 12.8 %collective-permute-start.3 = (bf16[832,128]{1,0:T(8,128)(2,1)}, bf16[832,128]{1,0:T(8,128)(2,1)S(1)}, u32[]{:S(2)}, u32[]{:S(2)}) collective-permute-start(bf16[832,128]{1,0:T(8,128)(2,1)} %get-tuple-element.56.refs_0_), channel_id=1, source_target_pairs={{0,4},{4,0},{8,12},{12,8},{16,20},{20,16},{24,28},{28,24},{1,5},{5... | collective-permute-start | bytes 638984 | tf_op jit(solution)/shard_map/ppermute | solution.py:411
  6.7 12.2 %collective-permute-start.2 = (bf16[832,128]{1,0:T(8,128)(2,1)}, bf16[832,128]{1,0:T(8,128)(2,1)S(1)}, u32[]{:S(2)}, u32[]{:S(2)}) collective-permute-start(bf16[832,128]{1,0:T(8,128)(2,1)} %get-tuple-element.56.refs_0_), channel_id=1, source_target_pairs={{0,16},{4,20},{8,24},{12,28},{16,0},{20,4},{24,8},{28,12},{1,17},{... | collective-permute-start | bytes 638984 | tf_op jit(solution)/shard_map/ppermute | solution.py:445
  9.3 2.0 %collective-permute-start = (bf16[96,128]{1,0:T(8,128)(2,1)}, bf16[96,128]{1,0:T(8,128)(2,1)S(1)}, u32[]{:S(2)}, u32[]{:S(2)}) collective-permute-start(bf16[96,128]{1,0:T(8,128)(2,1)} %get-tuple-element.52.coords), channel_id=1, source_target_pairs={{0,1},{1,0},{2,3},{3,2},{4,5},{5,4},{6,7},{7,6},{8,9},{9,8},{10,11... | collective-permute-start | bytes 73736 | tf_op jit(solution)/shard_map/ppermute | solution.py:411
  11.3 0.7 %copy-start.3 = (bf16[96,128]{1,0:T(8,128)(2,1)S(1)}, bf16[96,128]{1,0:T(8,128)(2,1)}, u32[]{:S(2)}) copy-start(bf16[96,128]{1,0:T(8,128)(2,1)} %get-tuple-element.52.coords) | copy-start | bytes 73732
  12.4 9.1 %copy-start.2 = (bf16[832,128]{1,0:T(8,128)(2,1)S(1)}, bf16[832,128]{1,0:T(8,128)(2,1)}, u32[]{:S(2)}) copy-start(bf16[832,128]{1,0:T(8,128)(2,1)} %get-tuple-element.56.refs_0_) | copy-start | bytes 638980
  13.5 8.0 %collective-permute-start.6 = (bf16[832,128]{1,0:T(8,128)(2,1)S(1)}, bf16[832,128]{1,0:T(8,128)(2,1)S(1)}, u32[]{:S(2)}, u32[]{:S(2)}) collective-permute-start(bf16[832,128]{1,0:T(8,128)(2,1)S(1)} %tie.4.refs_2_), channel_id=1, source_target_pairs={{0,4},{4,0},{8,12},{12,8},{16,20},{20,16},{24,28},{28,24},{1,5},{5... | collective-permute-start | bytes 638984 | tf_op jit(solution)/shard_map/ppermute | solution.py:411
  16.6 4.1 %collective-permute-start.1 = (bf16[192,128]{1,0:T(8,128)(2,1)S(1)}, bf16[192,128]{1,0:T(8,128)(2,1)S(1)}, u32[]{:S(2)}, u32[]{:S(2)}) collective-permute-start(bf16[192,128]{1,0:T(8,128)(2,1)S(1)} %get-tuple-element.55.refs_0_), channel_id=1, source_target_pairs={{0,2},{1,3},{2,0},{3,1},{4,6},{5,7},{6,4},{7,5},{8,10},{9,11},{10,... | collective-permute-start | bytes 147464 | tf_op jit(solution)/shard_map/ppermute | solution.py:411
  18.9 5.8 %collective-permute-start.5 = (bf16[832,128]{1,0:T(8,128)(2,1)S(1)}, bf16[832,128]{1,0:T(8,128)(2,1)S(1)}, u32[]{:S(2)}, u32[]{:S(2)}) collective-permute-start(bf16[832,128]{1,0:T(8,128)(2,1)S(1)} %tie.5.refs_2_.refs_4_), channel_id=1, source_target_pairs={{0,8},{4,12},{8,0},{12,4},{16,24},{20,28},{24,16},{28,20},{1,9},{5... | collective-permute-start | bytes 638984 | tf_op jit(solution)/shard_map/ppermute | solution.py:445
  18.9 9.1 %collective-permute-start.8 = (bf16[832,128]{1,0:T(8,128)(2,1)S(1)}, bf16[832,128]{1,0:T(8,128)(2,1)S(1)}, u32[]{:S(2)}, u32[]{:S(2)}) collective-permute-start(bf16[832,128]{1,0:T(8,128)(2,1)S(1)} %tie.5.refs_2_.refs_4_), channel_id=1, source_target_pairs={{0,4},{4,0},{8,12},{12,8},{16,20},{20,16},{24,28},{28,24},{1,5},{5... | collective-permute-start | bytes 638984 | tf_op jit(solution)/shard_map/ppermute | solution.py:411
  24.8 5.8 %collective-permute-start.7 = (bf16[832,128]{1,0:T(8,128)(2,1)S(1)}, bf16[832,128]{1,0:T(8,128)(2,1)S(1)}, u32[]{:S(2)}, u32[]{:S(2)}) collective-permute-start(bf16[832,128]{1,0:T(8,128)(2,1)S(1)} %tie.6.refs_1_), channel_id=1, source_target_pairs={{0,4},{4,0},{8,12},{12,8},{16,20},{20,16},{24,28},{28,24},{1,5},{5... | collective-permute-start | bytes 638984 | tf_op jit(solution)/shard_map/ppermute | solution.py:411
  32.9 1.5 %collective-permute-start.9 = (bf16[736,128]{1,0:T(8,128)(2,1)S(1)}, bf16[736,128]{1,0:T(8,128)(2,1)S(1)}, u32[]{:S(2)}, u32[]{:S(2)}) collective-permute-start(bf16[736,128]{1,0:T(8,128)(2,1)S(1)} %get-tuple-element.87), channel_id=1, source_target_pairs={{0,1},{1,0},{2,3},{3,2},{4,5},{5,4},{6,7},{7,6},{8,9},{9,8},{10,11... | collective-permute-start | bytes 565256 | tf_op jit(solution)/shard_map/ppermute | solution.py:411
  34.4 6.8 %collective-permute-start.10 = (bf16[736,128]{1,0:T(8,128)(2,1)S(1)}, bf16[736,128]{1,0:T(8,128)(2,1)S(1)}, u32[]{:S(2)}, u32[]{:S(2)}) collective-permute-start(bf16[736,128]{1,0:T(8,128)(2,1)S(1)} %join.1.refs_6_), channel_id=1, source_target_pairs={{0,2},{1,3},{2,0},{3,1},{4,6},{5,7},{6,4},{7,5},{8,10},{9,11},{10,... | collective-permute-start | bytes 565256 | tf_op jit(solution)/shard_map/ppermute | solution.py:411
  39.4 1.9 %copy-start = (bf16[1024,64]{0,1:T(8,128)(2,1)S(1)}, bf16[1024,64]{0,1:T(8,128)(2,1)}, u32[]{:S(2)}) copy-start(bf16[1024,64]{0,1:T(8,128)(2,1)} %param.12) | copy-start | bytes 393220
  39.4 1.8 %copy-start.1 = (bf16[384,64]{0,1:T(8,128)(2,1)S(1)}, bf16[384,64]{0,1:T(8,128)(2,1)}, u32[]{:S(2)}) copy-start(bf16[384,64]{0,1:T(8,128)(2,1)} %param.13) | copy-start | bytes 147460
  39.5 1.8 %collective-permute-start.11 = (bf16[736,128]{1,0:T(8,128)(2,1)S(1)}, bf16[736,128]{1,0:T(8,128)(2,1)S(1)}, u32[]{:S(2)}, u32[]{:S(2)}) collective-permute-start(bf16[736,128]{1,0:T(8,128)(2,1)S(1)} %get-tuple-element.98), channel_id=1, source_target_pairs={{0,1},{1,0},{2,3},{3,2},{4,5},{5,4},{6,7},{7,6},{8,9},{9,8},{10,11... | collective-permute-start | bytes 565256 | tf_op jit(solution)/shard_map/ppermute | solution.py:411

commit v2 on v1

--- a/solution.py
+++ b/solution.py
@@ -270,7 +270,9 @@
     far_from, far_count = bounds(1, FAR_UNROLL)
     halves = (near_count + half - 1) // half
     near_groups = halves // 2
-    far_groups = (far_count + FAR_UNROLL - 1) // FAR_UNROLL
+    far_half = FAR_UNROLL // 2
+    far_halves = (far_count + far_half - 1) // far_half
+    far_groups = far_halves // 2
     together = jnp.minimum(near_groups, far_groups)
     near_place = here * plan.near + near_from * NEAR_UNROLL
     far_place = plan.far_first + here * plan.far + far_from * FAR_UNROLL
@@ -302,6 +304,11 @@
     def _():
         for u in range(half):
             near_slot(near_place + near_groups * NEAR_UNROLL + u)
+
+    @pl.when(far_halves % 2 == 1)
+    def _():
+        for u in range(0, far_half, 2):
+            far_pair(far_place + far_groups * FAR_UNROLL + u)
 
 
 def write_parts(outs, near_total, far_even, far_odd):

time: 43 us -> 43.8 us (1.019); the launches traced: 42.7 us -> 44.1 us
  Pallas kernels: 14.6 us -> 18.7 us
  waiting for transfers between devices: 9.37 us -> 7.37 us
  starting transfers between devices: 15.9 us -> 15.1 us
    pallas_call x4, Pallas kernels: 6.82 us -> 9.81 us  [stage(): pl.pallas_call(functools.partial(kernel, plan, copied, members), out_shap...]
    ppermute x9, waiting for transfers between devices: 5.9 us -> 4.45 us  [exchange(): return lax.ppermute(x, axis, [(i, i ^ offset) for i in range(size)])]
    pallas_call x1, Pallas kernels: 3.28 us -> 4.33 us  [local(): pl.pallas_call(functools.partial(here_kernel, plan, copied), out_shape=lo...]
    ppermute x9, starting transfers between devices: 10.3 us -> 9.53 us  [exchange(): return lax.ppermute(x, axis, [(i, i ^ offset) for i in range(size)])]
    ppermute x3, waiting for transfers between devices: 3.47 us -> 2.92 us  [along_z(): return lax.ppermute(x, 'row', pairs)]
  transfers between devices with their start and end apart: 12 -> 12, of which waited for: 8 -> 9; matrix products, arithmetic and copies ran while one was open for 2% -> 2% of each run, Pallas kernels for 20% -> 28%
where the time goes in v2:
time: 43.8 us; the launch traced here: 44.1 us
  Pallas kernels  18.7 us (43%)
  starting transfers between devices  15.1 us (34%)
  waiting for transfers between devices  7.37 us (17%)
  between operations  1.41 us (3%)
  local copies, waits for them, and re-layouts  0.75 us (2%)
  other arithmetic  0.71 us (2%)
    pallas_call x4, Pallas kernels, stage(): pl.pallas_call(functools.partial(kernel, plan, copied, members), out_shap...  9.81 us
    ppermute x9, starting transfers between devices, exchange(): return lax.ppermute(x, axis, [(i, i ^ offset) for i in range(size)])  9.53 us
    ppermute x3, starting transfers between devices, along_z(): return lax.ppermute(x, 'row', pairs)  5.62 us
    ppermute x9, waiting for transfers between devices, exchange(): return lax.ppermute(x, axis, [(i, i ^ offset) for i in range(size)])  4.45 us
    pallas_call x1, Pallas kernels, local(): pl.pallas_call(functools.partial(here_kernel, plan, copied), out_shape=lo...  4.33 us
    ppermute x3, waiting for transfers between devices, along_z(): return lax.ppermute(x, 'row', pairs)  2.92 us
    pallas_call x1, Pallas kernels, local(): pl.pallas_call(pack_kernel, out_shape=[jax.ShapeDtypeStruct((PACKED_ROWS,...  2.17 us
    pallas_call x1, Pallas kernels, local(): pl.pallas_call(functools.partial(final_kernel, len(arrived)), out_shape=j...  1.44 us
  transfers between devices with their start and end apart: 12, of which 9 were waited for; matrix products, arithmetic and copies ran while one was open for 2% of the time, Pallas kernels for 28%

profile of v2, /device:TPU:0, one launch (start us, length us, event | category | flops | bytes accessed | tf_op | source)
XLA Modules:
  0.0 44.1 jit_solution(17041176602319406328)
XLA Ops:
  0.0 2.2 %pack.1 = (bf16[832,128]{1,0:T(8,128)(2,1)}, bf16[96,128]{1,0:T(8,128)(2,1)}) custom-call(bf16[64,1024]{1,0:T(8,128)(2,1)} %bitcast.10, bf16[64,1024]{1,0:T(8,128)(2,1)} %bitcast.6, bf16[64,384]{1,0:T(8,128)(2,1)} %bitcast.8, bf16[3,1024]{1,0:T(4,128)(2,1)} %points.1, bf16[3,448]{1,0:T(4,128)(2,1)} %skeleton.1), custom_call_target="tpu_custom_call" | custom-call | tf_op jit(solution)/shard_map/pack/pallas_call | solution.py:430
  2.2 3.0 %collective-permute-start.4 = (bf16[832,128]{1,0:T(8,128)(2,1)}, bf16[832,128]{1,0:T(8,128)(2,1)S(1)}, u32[]{:S(2)}, u32[]{:S(2)}) collective-permute-start(bf16[832,128]{1,0:T(8,128)(2,1)} %get-tuple-element.56.refs_0_), channel_id=1, source_target_pairs={{0,8},{4,12},{8,0},{12,4},{16,24},{20,28},{24,16},{28,20},{1,9},{5... | collective-permute-start | bytes 638984 | tf_op jit(solution)/shard_map/ppermute | solution.py:452
  5.2 1.5 %collective-permute-start.3 = (bf16[832,128]{1,0:T(8,128)(2,1)}, bf16[832,128]{1,0:T(8,128)(2,1)S(1)}, u32[]{:S(2)}, u32[]{:S(2)}) collective-permute-start(bf16[832,128]{1,0:T(8,128)(2,1)} %get-tuple-element.56.refs_0_), channel_id=1, source_target_pairs={{0,4},{4,0},{8,12},{12,8},{16,20},{20,16},{24,28},{28,24},{1,5},{5... | collective-permute-start | bytes 638984 | tf_op jit(solution)/shard_map/ppermute | solution.py:418
  6.7 2.6 %collective-permute-start.2 = (bf16[832,128]{1,0:T(8,128)(2,1)}, bf16[832,128]{1,0:T(8,128)(2,1)S(1)}, u32[]{:S(2)}, u32[]{:S(2)}) collective-permute-start(bf16[832,128]{1,0:T(8,128)(2,1)} %get-tuple-element.56.refs_0_), channel_id=1, source_target_pairs={{0,16},{4,20},{8,24},{12,28},{16,0},{20,4},{24,8},{28,12},{1,17},{... | collective-permute-start | bytes 638984 | tf_op jit(solution)/shard_map/ppermute | solution.py:452
  10.6 0.7 %pad_add_fusion.slots = s32[8,128]{1,0:T(8,128)S(1)} fusion(s32[1,1]{1,0:T(1,128)S(6)} %copy.79, s32[1,1]{1,0:T(1,128)S(6)} %copy.78, s32[2,128]{1,0:T(2,128)} %bitcast.11, s32[2,64]{1,0:T(2,128)} %bitcast.12), kind=kLoop, calls=%fused_computation | loop fusion | flops 3072 | bytes 5640 | tf_op jit(solution)/shard_map/add | solution.py:448
  11.3 0.7 %copy-done.3 = bf16[96,128]{1,0:T(8,128)(2,1)S(1)} copy-done((bf16[96,128]{1,0:T(8,128)(2,1)S(1)}, bf16[96,128]{1,0:T(8,128)(2,1)}, u32[]{:S(2)}) %copy-start.3) | copy-done | bytes 24600
  12.1 0.4 plan.1
  12.5 1.0 %collective-permute-done.4.refs_0_ = bf16[832,128]{1,0:T(8,128)(2,1)S(1)} collective-permute-done((bf16[832,128]{1,0:T(8,128)(2,1)}, bf16[832,128]{1,0:T(8,128)(2,1)S(1)}, u32[]{:S(2)}, u32[]{:S(2)}) %collective-permute-start.4) | collective-permute-done | bytes 213024 | tf_op jit(solution)/shard_map/ppermute | solution.py:452
  13.5 3.1 %collective-permute-start.6 = (bf16[832,128]{1,0:T(8,128)(2,1)S(1)}, bf16[832,128]{1,0:T(8,128)(2,1)S(1)}, u32[]{:S(2)}, u32[]{:S(2)}) collective-permute-start(bf16[832,128]{1,0:T(8,128)(2,1)S(1)} %tie.4.refs_2_), channel_id=1, source_target_pairs={{0,4},{4,0},{8,12},{12,8},{16,20},{20,16},{24,28},{28,24},{1,5},{5... | collective-permute-start | bytes 638984 | tf_op jit(solution)/shard_map/ppermute | solution.py:418
  16.6 1.5 %collective-permute-start.1 = (bf16[192,128]{1,0:T(8,128)(2,1)S(1)}, bf16[192,128]{1,0:T(8,128)(2,1)S(1)}, u32[]{:S(2)}, u32[]{:S(2)}) collective-permute-start(bf16[192,128]{1,0:T(8,128)(2,1)S(1)} %get-tuple-element.55.refs_0_), channel_id=1, source_target_pairs={{0,2},{1,3},{2,0},{3,1},{4,6},{5,7},{6,4},{7,5},{8,10},{9,11},{10,... | collective-permute-start | bytes 147464 | tf_op jit(solution)/shard_map/ppermute | solution.py:418
  18.0 0.9 %collective-permute-done.2.refs_0_ = bf16[832,128]{1,0:T(8,128)(2,1)S(1)} collective-permute-done((bf16[832,128]{1,0:T(8,128)(2,1)}, bf16[832,128]{1,0:T(8,128)(2,1)S(1)}, u32[]{:S(2)}, u32[]{:S(2)}) %collective-permute-start.2) | collective-permute-done | bytes 213024 | tf_op jit(solution)/shard_map/ppermute | solution.py:452
  18.9 0.7 %collective-permute-start.8 = (bf16[832,128]{1,0:T(8,128)(2,1)S(1)}, bf16[832,128]{1,0:T(8,128)(2,1)S(1)}, u32[]{:S(2)}, u32[]{:S(2)}) collective-permute-start(bf16[832,128]{1,0:T(8,128)(2,1)S(1)} %tie.5.refs_2_.refs_4_), channel_id=1, source_target_pairs={{0,4},{4,0},{8,12},{12,8},{16,20},{20,16},{24,28},{28,24},{1,5},{5... | collective-permute-start | bytes 638984 | tf_op jit(solution)/shard_map/ppermute | solution.py:418
  19.6 1.0 %collective-permute-done.1.refs_1_ = bf16[192,128]{1,0:T(8,128)(2,1)S(1)} collective-permute-done((bf16[192,128]{1,0:T(8,128)(2,1)S(1)}, bf16[192,128]{1,0:T(8,128)(2,1)S(1)}, u32[]{:S(2)}, u32[]{:S(2)}) %collective-permute-start.1) | collective-permute-done | bytes 49184 | tf_op jit(solution)/shard_map/ppermute | solution.py:418
  20.6 0.5 %row_side.1 = (bf16[18,256,16]{2,1,0:T(8,128)(2,1)S(1)}, bf16[30,64,16]{2,1,0:T(8,128)(2,1)S(1)}) custom-call(bf16[192,128]{1,0:T(8,128)(2,1)S(1)} %get-tuple-element.55.refs_0_, bf16[192,128]{1,0:T(8,128)(2,1)S(1)} %collective-permute-done.1.refs_1_, bf16[832,128]{1,0:T(8,128)(2,1)S(1)} %tie.5.refs_2_.refs_4_), custom_call_target="tpu_custom_call" | custom-call | tf_op jit(solution)/shard_map/row_side/pallas_call | solution.py:481
  21.1 0.4 collective-permute-done.6.refs_3_
  21.5 2.2 %early.1 = (bf16[32,64,256]{2,1,0:T(8,128)(2,1)S(1)}, bf16[32,16,256]{2,1,0:T(8,128)(2,1)S(1)}, bf16[56,64,128]{2,1,0:T(8,128)(2,1)S(1)}, bf16[56,64,128]{2,1,0:...) custom-call(s32[2,640]{1,0:T(2,128)S(1)} %get-tuple-element.53.refs_, ...), custom_call_target="tpu_custom_call" | custom-call | flops 8589934592 | bytes 1048576 | tf_op jit(solution)/shard_map/early/pallas_call | solution.py:518
  23.7 1.0 %collective-permute-done.5.refs_0_ = bf16[832,128]{1,0:T(8,128)(2,1)S(1)} collective-permute-done((bf16[832,128]{1,0:T(8,128)(2,1)S(1)}, bf16[832,128]{1,0:T(8,128)(2,1)S(1)}, u32[]{:S(2)}, u32[]{:S(2)}) %collective-permute-start.5) | collective-permute-done | bytes 213024 | tf_op jit(solution)/shard_map/ppermute | solution.py:452
  24.8 0.6 %collective-permute-start.7 = (bf16[832,128]{1,0:T(8,128)(2,1)S(1)}, bf16[832,128]{1,0:T(8,128)(2,1)S(1)}, u32[]{:S(2)}, u32[]{:S(2)}) collective-permute-start(bf16[832,128]{1,0:T(8,128)(2,1)S(1)} %tie.6.refs_1_), channel_id=1, source_target_pairs={{0,4},{4,0},{8,12},{12,8},{16,20},{20,16},{24,28},{28,24},{1,5},{5... | collective-permute-start | bytes 638984 | tf_op jit(solution)/shard_map/ppermute | solution.py:418
  25.4 3.8 %second.1 = (bf16[32,64,256]{2,1,0:T(8,128)(2,1)S(1)}, bf16[32,16,256]{2,1,0:T(8,128)(2,1)S(1)}, bf16[56,64,128]{2,1,0:T(8,128)(2,1)S(1)}, bf16[56,64,128]{2,1,0...) custom-call(s32[2,640]{1,0:T(2,128)S(1)} %get-tuple-element.53.refs_, ...), custom_call_target="tpu_custom_call", output_to_operand_aliasing={{0}: (4, {}), {1}: (5, {}), {2}: (6, {}), {3}: (7, {}), {4}... | custom-call | flops 8589934592 | bytes 1048576 | tf_op jit(solution)/shard_map/second/pallas_call | solution.py:518
  29.2 1.3 %mid.1 = (bf16[32,64,256]{2,1,0:T(8,128)(2,1)S(1)}, bf16[32,16,256]{2,1,0:T(8,128)(2,1)S(1)}, bf16[56,64,128]{2,1,0:T(8,128)(2,1)S(1)}, bf16[56,64,128]{2,1,0:T(...) custom-call(s32[2,640]{1,0:T(2,128)S(1)} %get-tuple-element.53.refs_, ...), custom_call_target="tpu_custom_call", output_to_operand_aliasing={{0}: (6, {}), {1}: (7, {}), {2}: (8, {}), {3}: (9, {}), {4}... | custom-call | flops 8589934592 | bytes 1048576 | tf_op jit(solution)/shard_map/mid/pallas_call | solution.py:518
  30.4 0.2 collective-permute-done.7.refs_0_
  30.6 2.6 %late.1 = (bf16[32,64,256]{2,1,0:T(8,128)(2,1)S(1)}, bf16[32,16,256]{2,1,0:T(8,128)(2,1)S(1)}, bf16[56,64,128]{2,1,0:T(8,128)(2,1)S(1)}, bf16[56,64,128]{2,1,0:T...) custom-call(s32[2,640]{1,0:T(2,128)S(1)} %get-tuple-element.53.refs_, ...), custom_call_target="tpu_custom_call", output_to_operand_aliasing={{0}: (5, {}), {1}: (6, {}), {2}: (7, {}), {3}: (8, {}), {4}... | custom-call | flops 8589934592 | bytes 1048576 | tf_op jit(solution)/shard_map/late/pallas_call | solution.py:518
  33.2 0.1 collective-permute-start.9
  33.3 1.4 %collective-permute-done.9.refs_1_ = bf16[736,128]{1,0:T(8,128)(2,1)S(1)} collective-permute-done((bf16[736,128]{1,0:T(8,128)(2,1)S(1)}, bf16[736,128]{1,0:T(8,128)(2,1)S(1)}, u32[]{:S(2)}, u32[]{:S(2)}) %collective-permute-start.9) | collective-permute-done | bytes 188448 | tf_op jit(solution)/shard_map/ppermute | solution.py:418
  34.7 0.1 join.1.refs_6_
  34.7 2.0 %collective-permute-start.10 = (bf16[736,128]{1,0:T(8,128)(2,1)S(1)}, bf16[736,128]{1,0:T(8,128)(2,1)S(1)}, u32[]{:S(2)}, u32[]{:S(2)}) collective-permute-start(bf16[736,128]{1,0:T(8,128)(2,1)S(1)} %join.1.refs_6_), channel_id=1, source_target_pairs={{0,2},{1,3},{2,0},{3,1},{4,6},{5,7},{6,4},{7,5},{8,10},{9,11},{10,... | collective-permute-start | bytes 565256 | tf_op jit(solution)/shard_map/ppermute | solution.py:418
  36.8 4.3 %here.1 = (f32[9,64,256]{2,1,0:T(8,128)S(1)}, f32[15,64,128]{2,1,0:T(8,128)S(1)}, f32[15,64,128]{2,1,0:T(8,128)S(1)}, bf16[736,128]{1,0:T(8,128)(2,1)S(1)}, bf16[736,128]{1,0:T(8,128)(2,1)S(1)}) custom-call(s32[2,640]{1,0:T(2,128)S(1)} %get-tuple-element.53.refs_1_.refs_3_.lists, ...), custom_call_target="tpu_custom_call", output_to_operand_aliasing={{0}: (11, {}), {1}: (12, {}), {2}: (13, {})} | custom-call | flops 8589934592 | bytes 1048576 | tf_op jit(solution)/shard_map/here/pallas_call | solution.py:548
  41.1 0.0 copy-start
  41.1 0.1 collective-permute-start.11
  41.2 0.6 %collective-permute-done.10.refs_0_ = bf16[736,128]{1,0:T(8,128)(2,1)S(1)} collective-permute-done((bf16[736,128]{1,0:T(8,128)(2,1)S(1)}, bf16[736,128]{1,0:T(8,128)(2,1)S(1)}, u32[]{:S(2)}, u32[]{:S(2)}) %collective-permute-start.10) | collective-permute-done | bytes 188448 | tf_op jit(solution)/shard_map/ppermute | solution.py:418
  41.8 0.8 %collective-permute-done.11.refs_2_ = bf16[736,128]{1,0:T(8,128)(2,1)S(1)} collective-permute-done((bf16[736,128]{1,0:T(8,128)(2,1)S(1)}, bf16[736,128]{1,0:T(8,128)(2,1)S(1)}, u32[]{:S(2)}, u32[]{:S(2)}) %collective-permute-start.11) | collective-permute-done | bytes 188448 | tf_op jit(solution)/shard_map/ppermute | solution.py:418
  42.6 1.4 %final.1 = bf16[64,1024]{1,0:T(8,128)(2,1)} custom-call(bf16[64,1024]{1,0:T(8,128)(2,1)S(1)} %bitcast.7, bf16[64,384]{1,0:T(8,128)(2,1)S(1)} %bitcast.9, bf16[736,128]{1,0:T(8,128)(2,1)S(1)} %tie.7.refs_0_, bf16[736,128]{1,0:T(8,128)(2,1)S(1)} %get-tuple-element.97.refs_1_, bf16[736,128]{1,0:T(8,128)(2,1)S(1)} %collective-permute-done.11.refs_2_), custom_call_target="tpu_custom_call" | custom-call | tf_op jit(solution)/shard_map/final/pallas_call | solution.py:560
  (15 shorter events, 0.0 us)
Async XLA Ops:
  2.2 11.3 %collective-permute-start.4 = (bf16[832,128]{1,0:T(8,128)(2,1)}, bf16[832,128]{1,0:T(8,128)(2,1)S(1)}, u32[]{:S(2)}, u32[]{:S(2)}) collective-permute-start(bf16[832,128]{1,0:T(8,128)(2,1)} %get-tuple-element.56.refs_0_), channel_id=1, source_target_pairs={{0,8},{4,12},{8,0},{12,4},{16,24},{20,28},{24,16},{28,20},{1,9},{5... | collective-permute-start | bytes 638984 | tf_op jit(solution)/shard_map/ppermute | solution.py:452
  5.2 12.8 %collective-permute-start.3 = (bf16[832,128]{1,0:T(8,128)(2,1)}, bf16[832,128]{1,0:T(8,128)(2,1)S(1)}, u32[]{:S(2)}, u32[]{:S(2)}) collective-permute-start(bf16[832,128]{1,0:T(8,128)(2,1)} %get-tuple-element.56.refs_0_), channel_id=1, source_target_pairs={{0,4},{4,0},{8,12},{12,8},{16,20},{20,16},{24,28},{28,24},{1,5},{5... | collective-permute-start | bytes 638984 | tf_op jit(solution)/shard_map/ppermute | solution.py:418
  6.7 12.2 %collective-permute-start.2 = (bf16[832,128]{1,0:T(8,128)(2,1)}, bf16[832,128]{1,0:T(8,128)(2,1)S(1)}, u32[]{:S(2)}, u32[]{:S(2)}) collective-permute-start(bf16[832,128]{1,0:T(8,128)(2,1)} %get-tuple-element.56.refs_0_), channel_id=1, source_target_pairs={{0,16},{4,20},{8,24},{12,28},{16,0},{20,4},{24,8},{28,12},{1,17},{... | collective-permute-start | bytes 638984 | tf_op jit(solution)/shard_map/ppermute | solution.py:452
  9.3 2.0 %collective-permute-start = (bf16[96,128]{1,0:T(8,128)(2,1)}, bf16[96,128]{1,0:T(8,128)(2,1)S(1)}, u32[]{:S(2)}, u32[]{:S(2)}) collective-permute-start(bf16[96,128]{1,0:T(8,128)(2,1)} %get-tuple-element.52.coords), channel_id=1, source_target_pairs={{0,1},{1,0},{2,3},{3,2},{4,5},{5,4},{6,7},{7,6},{8,9},{9,8},{10,11... | collective-permute-start | bytes 73736 | tf_op jit(solution)/shard_map/ppermute | solution.py:418
  11.3 0.7 %copy-start.3 = (bf16[96,128]{1,0:T(8,128)(2,1)S(1)}, bf16[96,128]{1,0:T(8,128)(2,1)}, u32[]{:S(2)}) copy-start(bf16[96,128]{1,0:T(8,128)(2,1)} %get-tuple-element.52.coords) | copy-start | bytes 73732
  12.4 9.1 %copy-start.2 = (bf16[832,128]{1,0:T(8,128)(2,1)S(1)}, bf16[832,128]{1,0:T(8,128)(2,1)}, u32[]{:S(2)}) copy-start(bf16[832,128]{1,0:T(8,128)(2,1)} %get-tuple-element.56.refs_0_) | copy-start | bytes 638980
  13.5 8.0 %collective-permute-start.6 = (bf16[832,128]{1,0:T(8,128)(2,1)S(1)}, bf16[832,128]{1,0:T(8,128)(2,1)S(1)}, u32[]{:S(2)}, u32[]{:S(2)}) collective-permute-start(bf16[832,128]{1,0:T(8,128)(2,1)S(1)} %tie.4.refs_2_), channel_id=1, source_target_pairs={{0,4},{4,0},{8,12},{12,8},{16,20},{20,16},{24,28},{28,24},{1,5},{5... | collective-permute-start | bytes 638984 | tf_op jit(solution)/shard_map/ppermute | solution.py:418
  16.6 4.1 %collective-permute-start.1 = (bf16[192,128]{1,0:T(8,128)(2,1)S(1)}, bf16[192,128]{1,0:T(8,128)(2,1)S(1)}, u32[]{:S(2)}, u32[]{:S(2)}) collective-permute-start(bf16[192,128]{1,0:T(8,128)(2,1)S(1)} %get-tuple-element.55.refs_0_), channel_id=1, source_target_pairs={{0,2},{1,3},{2,0},{3,1},{4,6},{5,7},{6,4},{7,5},{8,10},{9,11},{10,... | collective-permute-start | bytes 147464 | tf_op jit(solution)/shard_map/ppermute | solution.py:418
  18.9 5.8 %collective-permute-start.5 = (bf16[832,128]{1,0:T(8,128)(2,1)S(1)}, bf16[832,128]{1,0:T(8,128)(2,1)S(1)}, u32[]{:S(2)}, u32[]{:S(2)}) collective-permute-start(bf16[832,128]{1,0:T(8,128)(2,1)S(1)} %tie.5.refs_2_.refs_4_), channel_id=1, source_target_pairs={{0,8},{4,12},{8,0},{12,4},{16,24},{20,28},{24,16},{28,20},{1,9},{5... | collective-permute-start | bytes 638984 | tf_op jit(solution)/shard_map/ppermute | solution.py:452
  18.9 10.3 %collective-permute-start.8 = (bf16[832,128]{1,0:T(8,128)(2,1)S(1)}, bf16[832,128]{1,0:T(8,128)(2,1)S(1)}, u32[]{:S(2)}, u32[]{:S(2)}) collective-permute-start(bf16[832,128]{1,0:T(8,128)(2,1)S(1)} %tie.5.refs_2_.refs_4_), channel_id=1, source_target_pairs={{0,4},{4,0},{8,12},{12,8},{16,20},{20,16},{24,28},{28,24},{1,5},{5... | collective-permute-start | bytes 638984 | tf_op jit(solution)/shard_map/ppermute | solution.py:418
  24.8 5.8 %collective-permute-start.7 = (bf16[832,128]{1,0:T(8,128)(2,1)S(1)}, bf16[832,128]{1,0:T(8,128)(2,1)S(1)}, u32[]{:S(2)}, u32[]{:S(2)}) collective-permute-start(bf16[832,128]{1,0:T(8,128)(2,1)S(1)} %tie.6.refs_1_), channel_id=1, source_target_pairs={{0,4},{4,0},{8,12},{12,8},{16,20},{20,16},{24,28},{28,24},{1,5},{5... | collective-permute-start | bytes 638984 | tf_op jit(solution)/shard_map/ppermute | solution.py:418
  33.2 1.5 %collective-permute-start.9 = (bf16[736,128]{1,0:T(8,128)(2,1)S(1)}, bf16[736,128]{1,0:T(8,128)(2,1)S(1)}, u32[]{:S(2)}, u32[]{:S(2)}) collective-permute-start(bf16[736,128]{1,0:T(8,128)(2,1)S(1)} %get-tuple-element.87), channel_id=1, source_target_pairs={{0,1},{1,0},{2,3},{3,2},{4,5},{5,4},{6,7},{7,6},{8,9},{9,8},{10,11... | collective-permute-start | bytes 565256 | tf_op jit(solution)/shard_map/ppermute | solution.py:418
  34.7 7.1 %collective-permute-start.10 = (bf16[736,128]{1,0:T(8,128)(2,1)S(1)}, bf16[736,128]{1,0:T(8,128)(2,1)S(1)}, u32[]{:S(2)}, u32[]{:S(2)}) collective-permute-start(bf16[736,128]{1,0:T(8,128)(2,1)S(1)} %join.1.refs_6_), channel_id=1, source_target_pairs={{0,2},{1,3},{2,0},{3,1},{4,6},{5,7},{6,4},{7,5},{8,10},{9,11},{10,... | collective-permute-start | bytes 565256 | tf_op jit(solution)/shard_map/ppermute | solution.py:418
  41.1 1.5 %copy-start = (bf16[1024,64]{0,1:T(8,128)(2,1)S(1)}, bf16[1024,64]{0,1:T(8,128)(2,1)}, u32[]{:S(2)}) copy-start(bf16[1024,64]{0,1:T(8,128)(2,1)} %param.12) | copy-start | bytes 393220
  41.1 1.5 %copy-start.1 = (bf16[384,64]{0,1:T(8,128)(2,1)S(1)}, bf16[384,64]{0,1:T(8,128)(2,1)}, u32[]{:S(2)}) copy-start(bf16[384,64]{0,1:T(8,128)(2,1)} %param.13) | copy-start | bytes 147460
  41.1 1.5 %collective-permute-start.11 = (bf16[736,128]{1,0:T(8,128)(2,1)S(1)}, bf16[736,128]{1,0:T(8,128)(2,1)S(1)}, u32[]{:S(2)}, u32[]{:S(2)}) collective-permute-start(bf16[736,128]{1,0:T(8,128)(2,1)S(1)} %get-tuple-element.98), channel_id=1, source_target_pairs={{0,1},{1,0},{2,3},{3,2},{4,5},{5,4},{6,7},{7,6},{8,9},{9,8},{10,11... | collective-permute-start | bytes 565256 | tf_op jit(solution)/shard_map/ppermute | solution.py:418
